TPU v7x, 32 devices: a whole 2x2x4 slice. The times are simulated.
32 devices in a mesh: gx: 4 (over z), gy: 8 (over y, x, core).
Axes of the slice: x: 2, y: 2, z: 4, core: 2. Of those that a mesh axis runs over, the one named last changes fastest.
Arguments:
- probes: bfloat16 [3, 32, 384, 1024], P(None, None, 'gx', 'gy'), may hold values from -400 to 400
- depth: float32 [384, 1024], P('gx', 'gy'), may hold values from 0.5 to 2
- east_flow: float32 [384, 1024], P('gx', 'gy'), may hold values from -1 to 1
- north_flow: float32 [384, 1024], P('gx', 'gy'), may hold values from -1 to 1
- land_sea: int32 [384, 1024], P('gx', 'gy'), may hold values 0 or 1
Outputs:
- basis: bfloat16 [3, 32, 384, 1024], P(None, None, 'gx', 'gy')
- triangle: float32 [32, 32], replicated
Inputs may be any that keep to these rules, and one draw needn't show every extreme that they name: `land_sea`: 1 marks a sea cell, 0 a land cell.
All inputs are finite; a program needn't handle non-finite values. No bound on the sum of `land_sea` on one device may be relied on, other than what follows from the above.
Results may differ from a plain program's by a relative error of at most 0.001.
Values sent between devices are 32-bit elements; how exact they have to be, the bound alone decides.
No kernel may reach another device: no remote copies, remote signals or barrier semaphores. Data moves between devices by JAX's collectives and lax.ppermute only.
A program may use at most 128 MiB of HBM per device.

v0:
```python
import functools
import math

import jax
import jax.numpy as jnp
from jax import lax
from jax.experimental import pallas as pl
from jax.experimental.pallas import tpu as pltpu
from jax.sharding import PartitionSpec as P

STEPS = 2
HALO = 2 * STEPS
LANES = 128
TOP = 8

time_step = 0.3
coriolis = 0.5
gravity = 1.0

VMEM_LIMIT = 56 * 1024 * 1024


def lane_ids(rows):
    return lax.broadcasted_iota(jnp.int32, (rows, LANES), 1)


def pack_kernel(probes, depth, east_flow, north_flow, land_sea, x_low, x_high, y_low, y_high):
    fields, count, rows, _ = probes.shape
    lane = lane_ids(rows)
    sea = land_sea[...].astype(jnp.float32)

    def place(index, low, high, value):
        at = HALO * index
        turned = pltpu.roll(value, at, 1)
        low = jnp.where((lane >= at) & (lane < at + HALO), turned, low)
        back = lax.rem(at - HALO + LANES, LANES)
        high = jnp.where((lane >= back) & (lane < back + HALO), turned, high)
        return low, high

    zero = jnp.zeros((rows, LANES), jnp.float32)
    for c in range(fields):

        def body(p, carry):
            value = probes[c, p].astype(jnp.float32) * sea
            x_low[c * count + p] = value[:HALO]
            x_high[c * count + p] = value[rows - HALO :]
            return place(p, *carry, value)

        low, high = lax.fori_loop(0, count, body, (zero, zero))
        y_low[c] = low
        y_high[c] = high
    low, high = zero, zero
    for a, value in enumerate((depth[...], east_flow[...], north_flow[...], sea)):
        x_low[fields * count + a] = value[:HALO]
        x_high[fields * count + a] = value[rows - HALO :]
        low, high = place(jnp.int32(a), low, high, value)
    y_low[fields] = low
    y_high[fields] = high


def pack(probes, depth, east_flow, north_flow, land_sea):
    fields, count, rows, cols = probes.shape
    x_shape = jax.ShapeDtypeStruct((fields * count + 4, HALO, cols), jnp.float32)
    y_shape = jax.ShapeDtypeStruct((fields + 1, rows, LANES), jnp.float32)
    return pl.pallas_call(
        pack_kernel,
        out_shape=(x_shape, x_shape, y_shape, y_shape),
        compiler_params=pltpu.CompilerParams(vmem_limit_bytes=VMEM_LIMIT),
        name="pack_edges",
    )(probes, depth, east_flow, north_flow, land_sea)


def evolve_kernel(
    probes, depth, east_flow, north_flow, land_sea, x_before, x_after,
    y_before, y_own_high, y_own_low, y_after, c_before, c_after,
    halves, gram, coef, strip_coef, strips, edges, state, later, flux, grid_state, total,
):
    fields, count, rows, _ = probes.shape
    own = pl.ds(TOP, rows)
    bottom = TOP + rows
    tall = rows + 2 * HALO
    first = TOP - HALO
    tiles = [(first + 8 * t, 8) for t in range(tall // 8)]
    lane8 = lane_ids(8)
    half = 0.5 * time_step

    def fold(out, at, size, values):
        deep, east, north, sea = values
        out[0, pl.ds(at, size)] = deep
        out[1, pl.ds(at, size)] = half * sea * east
        out[2, pl.ds(at, size)] = half * sea * north
        out[3, pl.ds(at, size)] = (half * gravity) * sea

    base = fields * count
    sea = land_sea[...].astype(jnp.float32)
    fold(coef, TOP, rows, (depth[...], east_flow[...], north_flow[...], sea))
    fold(coef, first, HALO, [x_before[base + a] for a in range(4)])
    fold(coef, bottom, HALO, [x_after[base + a] for a in range(4)])

    kinds = (y_before, y_own_low, y_own_high, y_after)
    back = (HALO, 0, HALO, 0)

    def gathered(tile_of, size, slot_of):
        lane = lane_ids(size)
        part = lax.rem(lane, 16) // HALO
        out = None
        for k in range(4):
            index = (HALO * slot_of(lane) + lax.rem(lane, HALO) - back[k] + LANES) & (LANES - 1)
            picked = jnp.take_along_axis(tile_of(k), index, axis=1)
            out = picked if out is None else jnp.where(part == k, picked, out)
        return out

    groups = count // 8

    def unpack(at, size, tile_of):
        values = [
            gathered(lambda k: tile_of(k, fields), size, lambda lane: jnp.full_like(lane, a))
            for a in range(4)
        ]
        fold(strip_coef, at, size, values)
        for c in range(fields):
            for g in range(groups):
                strips[0, c, g, pl.ds(at, size)] = gathered(
                    lambda k: tile_of(k, c), size, lambda lane: 8 * g + lane // 16
                )

    for t in range(rows // 8):
        unpack(TOP + 8 * t, 8, lambda k, c: kinds[k][c, pl.ds(8 * t, 8)])
    whole = jnp.zeros((8 - HALO, LANES), jnp.float32)
    unpack(0, 8, lambda k, c: jnp.concatenate([whole, c_before[k, c]], 0))
    unpack(bottom, 8, lambda k, c: jnp.concatenate([c_after[k, c], whole], 0))

    def shifted(value, wrap):
        if wrap is None:
            return pltpu.roll(value, LANES - 1, 1) - pltpu.roll(value, 1, 1)
        up = jnp.where(lane8 == 0, wrap, value)
        down = jnp.where(lane8 == LANES - 1, wrap, value)
        return pltpu.roll(up, LANES - 1, 1) - pltpu.roll(down, 1, 1)

    def velocities(source, factors, wraps, write):
        for at, size in tiles:
            here, above, below = pl.ds(at, size), pl.ds(at - 1, size), pl.ds(at + 1, size)
            deep, east, north, slope = [factors[a, here] for a in range(4)]
            h, e, n = [source(c)[here] for c in range(3)]
            xh, xe, xn = [source(c)[below] - source(c)[above] for c in range(3)]
            yh, ye, yn = [shifted(v, wraps(c, here)) for c, v in enumerate((h, e, n))]
            e_new = e + (time_step * coriolis) * n - (east * xe + north * ye + slope * xh)
            n_new = n - (time_step * coriolis) * e - (east * xn + north * yn + slope * yh)
            write(at, e_new, n_new)
            flux[0, here] = deep * e_new
            flux[1, here] = deep * n_new
            flux[2, here] = h - (east * xh + north * yh)

    def heights(factors, wraps, write, spans):
        for at, size in spans:
            here, above, below = pl.ds(at, size), pl.ds(at - 1, size), pl.ds(at + 1, size)
            along = flux[0, below] - flux[0, above]
            across = shifted(flux[1, here], wraps(here))
            write(at, flux[2, here] - factors[3, here] * (along + across))

    def keep(slot, g, at, size, value):
        edges[slot, g, pl.ds(at, size)] = jnp.where(
            lax.rem(lane_ids(size), 16) == HALO, pltpu.roll(value, LANES - 8, 1), value
        )

    def strip_body(g, carry):
        for step in range(STEPS):
            for at, size in tiles:
                for c in range(fields):
                    keep(4 * step + c, g, at, size, strips[step, c, g, pl.ds(at, size)])

            def write_velocity(at, e_new, n_new):
                if step + 1 < STEPS:
                    strips[step + 1, 1, g, pl.ds(at, 8)] = e_new
                    strips[step + 1, 2, g, pl.ds(at, 8)] = n_new

            velocities(
                lambda c: strips.at[step, c, g], strip_coef, lambda c, here: None, write_velocity
            )
            for at, size in tiles:
                keep(4 * step + 3, g, at, size, flux[1, pl.ds(at, size)])
            if step + 1 < STEPS:

                def write_height(at, h_new):
                    strips[step + 1, 0, g, pl.ds(at, 8)] = h_new

                heights(strip_coef, lambda here: None, write_height, tiles)
        return carry

    lax.fori_loop(0, groups, strip_body, 0)

    def body(p, carry):
        group = p // 8
        turn = lax.rem(2 * LANES - 16 * lax.rem(p, 8) - HALO, LANES)
        for c in range(fields):
            state[c, own] = probes[c, p].astype(jnp.float32) * land_sea[...].astype(jnp.float32)
            state[c, pl.ds(first, HALO)] = x_before[c * count + p]
            state[c, pl.ds(bottom, HALO)] = x_after[c * count + p]

        def wrap(slot):
            return lambda here: pltpu.roll(edges[slot, group, here], turn, 1)

        def row(c):
            return pl.multiple_of((c * count + p) * rows, 8)

        buffers = (state, later)
        for step in range(STEPS):
            now = buffers[step]
            last = step + 1 == STEPS

            def write_velocity(at, e_new, n_new):
                if not last:
                    later[1, pl.ds(at, 8)] = e_new
                    later[2, pl.ds(at, 8)] = n_new
                else:
                    skip, keep_to = max(TOP - at, 0), min(bottom - at, 8)
                    span = pl.ds(row(1) + (at + skip - TOP), keep_to - skip)
                    grid_state[span] = e_new[skip:keep_to]
                    span = pl.ds(row(2) + (at + skip - TOP), keep_to - skip)
                    grid_state[span] = n_new[skip:keep_to]

            velocities(
                lambda c: now.at[c], coef, lambda c, here: wrap(4 * step + c)(here), write_velocity
            )

            def write_height(at, h_new):
                if not last:
                    later[0, pl.ds(at, 8)] = h_new
                else:
                    grid_state[pl.ds(row(0) + (at - TOP), 8)] = h_new

            spans = [(TOP + 8 * t, 8) for t in range(rows // 8)] if last else tiles
            heights(coef, wrap(4 * step + 3), write_height, spans)
        return carry

    lax.fori_loop(0, count, body, 0)

    total[...] = jnp.zeros_like(total)
    for c in range(fields):

        def gram_body(i, acc):
            pair = []
            for x in range(2):
                at = c * count * rows + 2 * i + x
                pair.append(grid_state[pl.ds(at, count, stride=rows)])
            values = jnp.concatenate(pair, 1)
            top = values.astype(jnp.bfloat16)
            low = (values - top.astype(jnp.float32)).astype(jnp.bfloat16)
            both = jnp.concatenate([top, low], 0)
            halves[c * (rows // 2) + i] = both
            return acc + lax.dot_general(
                both, both, (((1,), (1,)), ((), ())), preferred_element_type=jnp.float32
            )

        acc = lax.fori_loop(
            0, rows // 2, gram_body, jnp.zeros((2 * count, 2 * count), jnp.float32), unroll=8
        )
        total[:, : 2 * count] += acc
    value = total[...]
    summed = value[:count] + value[count:]
    summed = summed + pltpu.roll(summed, LANES - count, 1)
    lane = lane_ids(count)
    summed = jnp.where(lane < count, summed, 0.0)
    out = summed[:8]
    for b in range(1, count // 8):
        out = out + pltpu.roll(summed[8 * b : 8 * b + 8], count * b, 1)
    gram[...] = out


def evolve(probes, coefs, x_before, x_after, kinds, c_before, c_after):
    fields, count, rows, cols = probes.shape
    tall = rows + 2 * TOP
    groups = count // 8
    f32 = jnp.float32
    return pl.pallas_call(
        evolve_kernel,
        out_shape=(
            jax.ShapeDtypeStruct((fields * rows // 2, 2 * count, 2 * cols), jnp.bfloat16),
            jax.ShapeDtypeStruct((8, LANES), f32),
        ),
        scratch_shapes=[
            pltpu.VMEM((4, tall, LANES), f32),
            pltpu.VMEM((4, tall, LANES), f32),
            pltpu.VMEM((STEPS, fields, groups, tall, LANES), f32),
            pltpu.VMEM((4 * STEPS, groups, tall, LANES), f32),
            pltpu.VMEM((fields, tall, LANES), f32),
            pltpu.VMEM((fields, tall, LANES), f32),
            pltpu.VMEM((3, tall, LANES), f32),
            pltpu.VMEM((fields * count * rows, LANES), f32),
            pltpu.VMEM((2 * count, LANES), f32),
        ],
        compiler_params=pltpu.CompilerParams(vmem_limit_bytes=VMEM_LIMIT),
        name="evolve_and_gram",
    )(probes, *coefs, x_before, x_after, *kinds, c_before, c_after)


def finish_kernel(scale, grams, halves, basis, triangle, grid_out):
    fields, count, rows, cols = basis.shape
    summed = jnp.sum(grams[...], 0)
    lane = lane_ids(count)
    row_id = lax.broadcasted_iota(jnp.int32, (count, LANES), 0)
    gram = jnp.concatenate(
        [summed if b == 0 else pltpu.roll(summed, LANES - count * b, 1) for b in range(count // 8)],
        0,
    )
    work = jnp.where(lane < count, gram, jnp.where(lane == row_id + count, 1.0, 0.0))
    for k in range(count):
        pivot_row = work[k : k + 1]
        ratio = work[:, k : k + 1] / work[k : k + 1, k : k + 1]
        work = work - jnp.where(row_id > k, ratio * pivot_row, 0.0)
    pivots = jnp.sum(jnp.where(lane == row_id, work, 0.0), 1, keepdims=True)
    work = work / jnp.sqrt(pivots)
    triangle[...] = jnp.where(lane >= row_id, work, 0.0)[:, :count] * (1.0 / scale)
    lower = (work * scale)[:, count : 2 * count]
    top = lower.astype(jnp.bfloat16)
    low = (lower - top.astype(jnp.float32)).astype(jnp.bfloat16)
    factor = jnp.concatenate([top, top, low], 1)

    for c in range(fields):

        def body(i, carry):
            both = halves[c * (rows // 2) + i]
            stacked = jnp.concatenate([both, both[:count]], 0)
            out = jnp.dot(factor, stacked, preferred_element_type=jnp.float32)
            for x in range(2):
                grid_out[pl.ds(2 * i + x, count, stride=rows)] = out[:, x * cols : (x + 1) * cols]
            return carry

        lax.fori_loop(0, rows // 2, body, 0, unroll=8)

        def store(q, carry):
            at = pl.multiple_of(q * rows, 8)
            basis[c, q] = grid_out[pl.ds(at, rows)].astype(jnp.bfloat16)
            return carry

        lax.fori_loop(0, count, store, 0, unroll=4)


def finish(grams, halves, shape, scale):
    fields, count, rows, cols = shape
    return pl.pallas_call(
        functools.partial(finish_kernel, scale),
        out_shape=(
            jax.ShapeDtypeStruct(shape, jnp.bfloat16),
            jax.ShapeDtypeStruct((count, count), jnp.float32),
        ),
        scratch_shapes=[pltpu.VMEM((count * rows, cols), jnp.float32)],
        compiler_params=pltpu.CompilerParams(vmem_limit_bytes=VMEM_LIMIT),
        name="factor_and_apply",
    )(grams, halves)


def per_device(probes, depth, east_flow, north_flow, land_sea):
    fields, count, rows, cols = probes.shape
    nx, ny = lax.axis_size("gx"), lax.axis_size("gy")
    up_x = [(i, i + 1) for i in range(nx - 1)]
    down_x = [(j, i) for i, j in up_x]
    up_y = [(i, i + 1) for i in range(ny - 1)]
    down_y = [(j, i) for i, j in up_y]
    coefs = (depth, east_flow, north_flow, land_sea)
    x_low, x_high, y_low, y_high = pack(probes, *coefs)
    y_before = lax.ppermute(y_high, "gy", up_y)
    y_after = lax.ppermute(y_low, "gy", down_y)
    x_before = lax.ppermute(x_high, "gx", up_x)
    x_after = lax.ppermute(x_low, "gx", down_x)
    kinds = (y_before, y_low, y_high, y_after)
    c_before = lax.ppermute(jnp.stack([k[:, rows - HALO :] for k in kinds]), "gx", up_x)
    c_after = lax.ppermute(jnp.stack([k[:, :HALO] for k in kinds]), "gx", down_x)
    halves, gram = evolve(
        probes, coefs, x_before, x_after, (y_before, y_high, y_low, y_after), c_before, c_after
    )
    devices = nx * ny
    grams = lax.all_to_all(
        jnp.broadcast_to(gram[None], (devices,) + gram.shape), ("gx", "gy"), 0, 0
    )
    scale = math.sqrt(fields * rows * nx * cols * ny)
    return finish(grams, halves, probes.shape, scale)


def solution(mesh):
    in_specs = (
        P(None, None, "gx", "gy"),
        P("gx", "gy"),
        P("gx", "gy"),
        P("gx", "gy"),
        P("gx", "gy"),
    )
    out_specs = (P(None, None, "gx", "gy"), P())
    return jax.shard_map(
        per_device, mesh=mesh, in_specs=in_specs, out_specs=out_specs, check_vma=False
    )
```

profile of v0, /device:TPU:0, one launch (start us, length us, event | category | flops | bytes accessed | tf_op | source)
XLA Modules:
  0.0 149.3 jit_solution(18399994098961913019)
XLA Ops:
  0.6 10.5 %pack_edges.1 = (f32[100,4,128]{2,1,0:T(4,128)}, f32[100,4,128]{2,1,0:T(4,128)}, f32[4,96,128]{2,1,0:T(8,128)}, f32[4,96,128]{2,1,0:T(8,128)}) custom-call(bf16[3,32,96,128]{3,2,1,0:T(8,128)(2,1)} %probes.3, f32[96,128]{1,0:T(8,128)} %depth.3, f32[96,128]{1,0:T(8,128)} %east_flow.3, f32[96,128]{1,0:T(8,128)} %north_flow.3, s32[96,128]{1,0:T(8,128)} %land_sea.3), custom_call_target="tpu_custom_call" | custom-call | tf_op jit(solution)/shard_map/pack_edges/pallas_call | solution.py:65
  11.1 2.4 %collective-permute-start.2 = (f32[4,96,128]{2,1,0:T(8,128)}, f32[4,96,128]{2,1,0:T(8,128)S(1)}, u32[]{:S(2)}, u32[]{:S(2)}) collective-permute-start(f32[4,96,128]{2,1,0:T(8,128)} %get-tuple-element.10.y_own_high), channel_id=1, source_target_pairs={{0,1},{1,2},{2,3},{3,4},{4,5},{5,6},{6,7},{8,9},{9,10},{10,11},{11... | collective-permute-start | bytes 589832 | tf_op jit(solution)/shard_map/ppermute | solution.py:362
  13.5 1.3 collective-permute-start.3
  14.8 4.3 %collective-permute-start = (f32[100,4,128]{2,1,0:T(4,128)}, f32[100,4,128]{2,1,0:T(4,128)S(1)}, u32[]{:S(2)}, u32[]{:S(2)}) collective-permute-start(f32[100,4,128]{2,1,0:T(4,128)} %get-tuple-element.8), channel_id=1, source_target_pairs={{0,8},{8,16},{16,24},{1,9},{9,17},{17,25},{2,10},{10,18},{18,26},{... | collective-permute-start | bytes 614408 | tf_op jit(solution)/shard_map/ppermute | solution.py:364
  19.1 1.3 collective-permute-start.1
  20.4 0.8 slice_bitcast_fusion.4
  21.2 0.0 collective-permute-done.2.y_before
  21.2 0.0 copy-start
  21.2 0.0 collective-permute-done.3.y_after
  21.2 0.0 copy-start.1
  21.3 4.5 %collective-permute-start.4 = (f32[4,4,4,128]{3,2,1,0:T(4,128)S(1)}, f32[4,4,4,128]{3,2,1,0:T(4,128)S(1)}, u32[]{:S(2)}, u32[]{:S(2)}) collective-permute-start(f32[4,4,4,128]{3,2,1,0:T(4,128)S(1)} %pad_maximum_fusion), channel_id=1, source_target_pairs={{0,8},{8,16},{16,24},{1,9},{9,17},{17,25},{2,10},{10,18},{18,26},{... | collective-permute-start | bytes 98312 | tf_op jit(solution)/shard_map/ppermute | solution.py:367
  25.9 1.3 collective-permute-start.5
  27.2 0.0 collective-permute-done.x_before
  27.2 0.0 copy-start.2
  27.2 0.8 collective-permute-done.1.x_after
  28.0 0.0 copy-start.3
  28.0 0.0 collective-permute-done.4.c_before
  28.0 0.0 copy-start.4
  28.0 3.6 %collective-permute-done.5.c_after = f32[4,4,4,128]{3,2,1,0:T(4,128)S(1)} collective-permute-done((f32[4,4,4,128]{3,2,1,0:T(4,128)S(1)}, f32[4,4,4,128]{3,2,1,0:T(4,128)S(1)}, u32[]{:S(2)}, u32[]{:S(2)}) %collective-permute-start.5) | collective-permute-done | bytes 32800 | tf_op jit(solution)/shard_map/ppermute | solution.py:368
  31.7 0.0 copy-done
  31.7 0.0 copy-done.1
  31.7 0.0 copy-done.2
  31.7 0.0 copy-done.3
  31.7 0.0 copy-done.4
  31.7 0.0 copy-start.5
  31.7 0.6 copy-done.5
  32.3 89.0 %evolve_and_gram.1 = (bf16[144,64,256]{2,1,0:T(8,128)(2,1)}, f32[8,128]{1,0:T(8,128)}) custom-call(bf16[3,32,96,128]{3,2,1,0:T(8,128)(2,1)} %probes.3, f32[96,128]{1,0:T(8,128)} %depth.3, f32[96,128]{1,0:T(8,128)} %east_flow.3, f32[96,128]{1,0:T(8,128)} %north_flow.3, s32[96,128]{1,0:T(8,128)} %land_sea.3, f32[100,4,128]{2,1,0:T(4,128)} %copy-done.2, ...), custom_call_target="tpu_custom_call" | custom-call | tf_op jit(solution)/shard_map/evolve_and_gram/pallas_call | solution.py:275
  121.3 0.7 broadcast_in_dim.2
  122.0 15.5 %all_to_all.5.grams = f32[32,8,128]{2,1,0:T(8,128)} all-to-all(f32[32,8,128]{2,1,0:T(8,128)S(1)} %broadcast_in_dim.2), channel_id=1, replica_groups=mesh['gx'=4,'gy'=8] {'gx','gy'}, dimensions={0} | all-to-all | bytes 262144 | tf_op jit(solution)/shard_map/all_to_all | solution.py:373
  137.5 11.8 %factor_and_apply.1 = (bf16[3,32,96,128]{3,2,1,0:T(8,128)(2,1)}, f32[32,32]{1,0:T(8,128)}) custom-call(f32[32,8,128]{2,1,0:T(8,128)} %all_to_all.5.grams, bf16[144,64,256]{2,1,0:T(8,128)(2,1)} %get-tuple-element.13.halves), custom_call_target="tpu_custom_call" | custom-call | tf_op jit(solution)/shard_map/factor_and_apply/pallas_call | solution.py:341
  (4 shorter events, 0.0 us)
Async XLA Ops:
  11.1 10.1 %collective-permute-start.2 = (f32[4,96,128]{2,1,0:T(8,128)}, f32[4,96,128]{2,1,0:T(8,128)S(1)}, u32[]{:S(2)}, u32[]{:S(2)}) collective-permute-start(f32[4,96,128]{2,1,0:T(8,128)} %get-tuple-element.10.y_own_high), channel_id=1, source_target_pairs={{0,1},{1,2},{2,3},{3,4},{4,5},{5,6},{6,7},{8,9},{9,10},{10,11},{11... | collective-permute-start | bytes 589832 | tf_op jit(solution)/shard_map/ppermute | solution.py:362
  13.5 7.7 %collective-permute-start.3 = (f32[4,96,128]{2,1,0:T(8,128)}, f32[4,96,128]{2,1,0:T(8,128)S(1)}, u32[]{:S(2)}, u32[]{:S(2)}) collective-permute-start(f32[4,96,128]{2,1,0:T(8,128)} %get-tuple-element.11.y_own_low), channel_id=1, source_target_pairs={{1,0},{2,1},{3,2},{4,3},{5,4},{6,5},{7,6},{9,8},{10,9},{11,10},{12... | collective-permute-start | bytes 589832 | tf_op jit(solution)/shard_map/ppermute | solution.py:363
  14.8 12.4 %collective-permute-start = (f32[100,4,128]{2,1,0:T(4,128)}, f32[100,4,128]{2,1,0:T(4,128)S(1)}, u32[]{:S(2)}, u32[]{:S(2)}) collective-permute-start(f32[100,4,128]{2,1,0:T(4,128)} %get-tuple-element.8), channel_id=1, source_target_pairs={{0,8},{8,16},{16,24},{1,9},{9,17},{17,25},{2,10},{10,18},{18,26},{... | collective-permute-start | bytes 614408 | tf_op jit(solution)/shard_map/ppermute | solution.py:364
  19.1 8.9 %collective-permute-start.1 = (f32[100,4,128]{2,1,0:T(4,128)}, f32[100,4,128]{2,1,0:T(4,128)S(1)}, u32[]{:S(2)}, u32[]{:S(2)}) collective-permute-start(f32[100,4,128]{2,1,0:T(4,128)} %get-tuple-element.9), channel_id=1, source_target_pairs={{8,0},{16,8},{24,16},{9,1},{17,9},{25,17},{10,2},{18,10},{26,18},{... | collective-permute-start | bytes 614408 | tf_op jit(solution)/shard_map/ppermute | solution.py:365
  21.2 10.5 %copy-start = (f32[4,96,128]{2,1,0:T(8,128)}, f32[4,96,128]{2,1,0:T(8,128)S(1)}, u32[]{:S(2)}) copy-start(f32[4,96,128]{2,1,0:T(8,128)S(1)} %collective-permute-done.2.y_before) | copy-start | bytes 589828
  21.2 10.4 %copy-start.1 = (f32[4,96,128]{2,1,0:T(8,128)}, f32[4,96,128]{2,1,0:T(8,128)S(1)}, u32[]{:S(2)}) copy-start(f32[4,96,128]{2,1,0:T(8,128)S(1)} %collective-permute-done.3.y_after) | copy-start | bytes 589828
  21.3 6.7 %collective-permute-start.4 = (f32[4,4,4,128]{3,2,1,0:T(4,128)S(1)}, f32[4,4,4,128]{3,2,1,0:T(4,128)S(1)}, u32[]{:S(2)}, u32[]{:S(2)}) collective-permute-start(f32[4,4,4,128]{3,2,1,0:T(4,128)S(1)} %pad_maximum_fusion), channel_id=1, source_target_pairs={{0,8},{8,16},{16,24},{1,9},{9,17},{17,25},{2,10},{10,18},{18,26},{... | collective-permute-start | bytes 98312 | tf_op jit(solution)/shard_map/ppermute | solution.py:367
  25.9 5.8 %collective-permute-start.5 = (f32[4,4,4,128]{3,2,1,0:T(4,128)S(1)}, f32[4,4,4,128]{3,2,1,0:T(4,128)S(1)}, u32[]{:S(2)}, u32[]{:S(2)}) collective-permute-start(f32[4,4,4,128]{3,2,1,0:T(4,128)S(1)} %pad_maximum_fusion.1), channel_id=1, source_target_pairs={{8,0},{16,8},{24,16},{9,1},{17,9},{25,17},{10,2},{18,10},{26,18},{... | collective-permute-start | bytes 98312 | tf_op jit(solution)/shard_map/ppermute | solution.py:368
  27.2 4.5 %copy-start.2 = (f32[100,4,128]{2,1,0:T(4,128)}, f32[100,4,128]{2,1,0:T(4,128)S(1)}, u32[]{:S(2)}) copy-start(f32[100,4,128]{2,1,0:T(4,128)S(1)} %collective-permute-done.x_before) | copy-start | bytes 614404
  28.0 3.7 %copy-start.3 = (f32[100,4,128]{2,1,0:T(4,128)}, f32[100,4,128]{2,1,0:T(4,128)S(1)}, u32[]{:S(2)}) copy-start(f32[100,4,128]{2,1,0:T(4,128)S(1)} %collective-permute-done.1.x_after) | copy-start | bytes 614404
  28.0 3.7 %copy-start.4 = (f32[4,4,4,128]{3,2,1,0:T(4,128)}, f32[4,4,4,128]{3,2,1,0:T(4,128)S(1)}, u32[]{:S(2)}) copy-start(f32[4,4,4,128]{3,2,1,0:T(4,128)S(1)} %collective-permute-done.4.c_before) | copy-start | bytes 98308
  31.7 0.6 copy-start.5
where the time goes:
time: 150 us; the launch traced here: 149 us
  Pallas kernels  111 us (74%)
  blocking collectives  15.5 us (10%)
  starting transfers between devices  15.1 us (10%)
  waiting for transfers between devices  4.49 us (3%)
  local copies, waits for them, and re-layouts  2.1 us (1%)
    pallas_call x1, Pallas kernels, evolve(): pl.pallas_call(evolve_kernel, out_shape=(jax.ShapeDtypeStruct((fields * r...  89 us
    all_to_all x1, blocking collectives, per_device(): lax.all_to_all(jnp.broadcast_to(gram[None], (devices,) + gram.shape), ('g...  15.5 us
    pallas_call x1, Pallas kernels, finish(): pl.pallas_call(functools.partial(finish_kernel, scale), out_shape=(jax.Sh...  11.8 us
    pallas_call x1, Pallas kernels, pack(): pl.pallas_call(pack_kernel, out_shape=(x_shape, x_shape, y_shape, y_shape...  10.5 us
    ppermute x1, starting transfers between devices, per_device(): lax.ppermute(jnp.stack([k[:, rows - HALO:] for k in kinds]), 'gx', up_x)  4.55 us
    ppermute x1, starting transfers between devices, per_device(): x_before = lax.ppermute(x_high, 'gx', up_x)  4.32 us
    ppermute x1, waiting for transfers between devices, per_device(): lax.ppermute(jnp.stack([k[:, :HALO] for k in kinds]), 'gx', down_x)  3.65 us
  transfers between devices with their start and end apart: 6, of which 2 were waited for; matrix products, arithmetic and copies ran while one was open for 1% of the time, Pallas kernels for 0%

commit v1 on v0

v1 whole, which is shorter than its diff:
```python
import functools
import math

import jax
import jax.numpy as jnp
from jax import lax
from jax.experimental import pallas as pl
from jax.experimental.pallas import tpu as pltpu
from jax.sharding import PartitionSpec as P

STEPS = 2
HALO = 2 * STEPS
LANES = 128
TOP = 8

time_step = 0.3
coriolis = 0.5
gravity = 1.0

VMEM_LIMIT = 24 * 1024 * 1024
BLOCK = 8


def lane_ids(rows):
    return lax.broadcasted_iota(jnp.int32, (rows, LANES), 1)


def pack_kernel(
    probes, depth, east_flow, north_flow, land_sea,
    x_a, x_b, y_a, y_b, held, coefs, mask, sems,
):
    fields, count, rows, _ = held.shape
    even_x = lax.rem(lax.axis_index("gx"), 2) == 0
    even_y = lax.rem(lax.axis_index("gy"), 2) == 0
    small = [
        pltpu.make_async_copy(source, target, sems.at[fields + i])
        for i, (source, target) in enumerate(
            ((land_sea, mask), (depth, coefs.at[0]), (east_flow, coefs.at[1]), (north_flow, coefs.at[2]))
        )
    ]
    large = [
        pltpu.make_async_copy(probes.at[c], held.at[c], sems.at[c]) for c in range(fields)
    ]
    for copy in small + large:
        copy.start()
    for copy in small:
        copy.wait()
    lane = lane_ids(rows)
    coefs[3] = mask[...].astype(jnp.float32)

    def place(index, low, high, value):
        at = HALO * index
        turned = pltpu.roll(value, at, 1) if index else value
        low = jnp.where((lane >= at) & (lane < at + HALO), turned, low)
        back = (at - HALO) % LANES
        high = jnp.where((lane >= back) & (lane < back + HALO), turned, high)
        return low, high

    def rows_out(at, value):
        low, high = value[:HALO], value[rows - HALO :]
        x_a[at] = jnp.where(even_x, high, low)
        x_b[at] = jnp.where(even_x, low, high)

    def columns_out(at, low, high):
        y_a[at] = jnp.where(even_y, high, low)
        y_b[at] = jnp.where(even_y, low, high)

    zero = jnp.zeros((rows, LANES), jnp.float32)
    low, high = zero, zero
    for a in range(4):
        value = coefs[a]
        rows_out(fields * count + a, value)
        low, high = place(a, low, high, value)
    columns_out(fields, low, high)
    for c in range(fields):
        large[c].wait()
        low, high = zero, zero
        for p in range(count):
            value = held[c, p].astype(jnp.float32) * coefs[3]
            rows_out(c * count + p, value)
            low, high = place(p, low, high, value)
        columns_out(c, low, high)


def pack(probes, depth, east_flow, north_flow, land_sea):
    fields, count, rows, cols = probes.shape
    f32 = jnp.float32
    x_shape = jax.ShapeDtypeStruct((fields * count + 4, HALO, cols), f32)
    y_shape = jax.ShapeDtypeStruct((fields + 1, rows, LANES), f32)
    return pl.pallas_call(
        pack_kernel,
        in_specs=[pl.BlockSpec(memory_space=pltpu.HBM)] * 5,
        out_shape=(
            x_shape, x_shape, y_shape, y_shape,
            jax.ShapeDtypeStruct(probes.shape, probes.dtype),
            jax.ShapeDtypeStruct((4, rows, cols), f32),
        ),
        scratch_shapes=[
            pltpu.VMEM((rows, cols), jnp.int32),
            pltpu.SemaphoreType.DMA((fields + 4,)),
        ],
        compiler_params=pltpu.CompilerParams(vmem_limit_bytes=VMEM_LIMIT),
        name="pack_edges",
    )(probes, depth, east_flow, north_flow, land_sea)


def evolve_kernel(
    probes, coefs, x_a, x_b, to_a, to_b, from_a, from_b, c_a, c_b,
    halves, gram, coef, strip_coef, strips, edges, wraps_of, state, later, flux, grid_state, total,
):
    fields, count, rows, _ = probes.shape
    own = pl.ds(TOP, rows)
    bottom = TOP + rows
    tall = rows + 2 * HALO
    first = TOP - HALO
    tiles = [(first + 8 * t, 8) for t in range(tall // 8)]
    lane8 = lane_ids(8)
    half = 0.5 * time_step
    even_x = lax.rem(lax.axis_index("gx"), 2) == 0
    even_y = lax.rem(lax.axis_index("gy"), 2) == 0

    def x_before(i):
        return jnp.where(even_x, x_b[i], x_a[i])

    def x_after(i):
        return jnp.where(even_x, x_a[i], x_b[i])

    def fold(out, at, size, values):
        deep, east, north, sea = values
        out[0, pl.ds(at, size)] = deep
        out[1, pl.ds(at, size)] = half * sea * east
        out[2, pl.ds(at, size)] = half * sea * north
        out[3, pl.ds(at, size)] = (half * gravity) * sea

    base = fields * count
    fold(coef, TOP, rows, [coefs[a] for a in range(4)])
    fold(coef, first, HALO, [x_before(base + a) for a in range(4)])
    fold(coef, bottom, HALO, [x_after(base + a) for a in range(4)])

    def kinds(k, *at):
        mine, theirs = (to_b, to_a) if k in (1, 2) else (from_b, from_a)
        if k in (2, 3):
            mine, theirs = theirs, mine
        return jnp.where(even_y, mine[at], theirs[at])

    back = (HALO, 0, HALO, 0)

    def gathered(tile_of, size, slot_of):
        lane = lane_ids(size)
        part = lax.rem(lane, 16) // HALO
        out = None
        for k in range(4):
            index = (HALO * slot_of(lane) + lax.rem(lane, HALO) - back[k] + LANES) & (LANES - 1)
            picked = jnp.take_along_axis(tile_of(k), index, axis=1)
            out = picked if out is None else jnp.where(part == k, picked, out)
        return out

    groups = count // 8

    def unpack(at, size, tile_of):
        values = [
            gathered(lambda k: tile_of(k, fields), size, lambda lane: jnp.full_like(lane, a))
            for a in range(4)
        ]
        fold(strip_coef, at, size, values)
        for c in range(fields):
            for g in range(groups):
                strips[0, c, g, pl.ds(at, size)] = gathered(
                    lambda k: tile_of(k, c), size, lambda lane: 8 * g + lane // 16
                )

    for t in range(rows // 8):
        unpack(TOP + 8 * t, 8, lambda k, c: kinds(k, c, pl.ds(8 * t, 8)))
    whole = jnp.zeros((8 - HALO, LANES), jnp.float32)
    unpack(0, 8, lambda k, c: jnp.concatenate([whole, jnp.where(even_x, c_b[k, c], c_a[k, c])], 0))
    unpack(bottom, 8, lambda k, c: jnp.concatenate([jnp.where(even_x, c_a[k, c], c_b[k, c]), whole], 0))

    def shifted(value, wrap):
        if wrap is None:
            return pltpu.roll(value, LANES - 1, 1) - pltpu.roll(value, 1, 1)
        up = jnp.where(lane8 == 0, wrap, value)
        down = jnp.where(lane8 == LANES - 1, wrap, value)
        return pltpu.roll(up, LANES - 1, 1) - pltpu.roll(down, 1, 1)

    def velocities(source, factors, wraps, write):
        for at, size in tiles:
            here, above, below = pl.ds(at, size), pl.ds(at - 1, size), pl.ds(at + 1, size)
            deep, east, north, slope = [factors[a, here] for a in range(4)]
            h, e, n = [source(c)[here] for c in range(3)]
            xh, xe, xn = [source(c)[below] - source(c)[above] for c in range(3)]
            yh, ye, yn = [shifted(v, wraps(c, here)) for c, v in enumerate((h, e, n))]
            e_new = e + (time_step * coriolis) * n - (east * xe + north * ye + slope * xh)
            n_new = n - (time_step * coriolis) * e - (east * xn + north * yn + slope * yh)
            write(at, e_new, n_new)
            flux[0, here] = deep * e_new
            flux[1, here] = deep * n_new
            flux[2, here] = h - (east * xh + north * yh)

    def heights(factors, wraps, write):
        for at, size in tiles:
            here, above, below = pl.ds(at, size), pl.ds(at - 1, size), pl.ds(at + 1, size)
            along = flux[0, below] - flux[0, above]
            across = shifted(flux[1, here], wraps(here))
            write(at, flux[2, here] - factors[3, here] * (along + across))

    def keep(slot, g, at, size, value):
        edges[slot, g, pl.ds(at, size)] = jnp.where(
            lax.rem(lane_ids(size), 16) == HALO, pltpu.roll(value, LANES - 8, 1), value
        )

    def strip_body(g, carry):
        for step in range(STEPS):
            for at, size in tiles:
                for c in range(fields):
                    keep(4 * step + c, g, at, size, strips[step, c, g, pl.ds(at, size)])

            def write_velocity(at, e_new, n_new):
                if step + 1 < STEPS:
                    strips[step + 1, 1, g, pl.ds(at, 8)] = e_new
                    strips[step + 1, 2, g, pl.ds(at, 8)] = n_new

            velocities(
                lambda c: strips.at[step, c, g], strip_coef, lambda c, here: None, write_velocity
            )
            for at, size in tiles:
                keep(4 * step + 3, g, at, size, flux[1, pl.ds(at, size)])
            if step + 1 < STEPS:

                def write_height(at, h_new):
                    strips[step + 1, 0, g, pl.ds(at, 8)] = h_new

                heights(strip_coef, lambda here: None, write_height)
        return carry

    lax.fori_loop(0, groups, strip_body, 0)

    def body(p, carry):
        group = p // 8
        turn = lax.rem(2 * LANES - 16 * lax.rem(p, 8) - HALO, LANES)
        for c in range(fields):
            state[c, own] = probes[c, p].astype(jnp.float32) * coefs[3]
            state[c, pl.ds(first, HALO)] = x_before(c * count + p)
            state[c, pl.ds(bottom, HALO)] = x_after(c * count + p)
        for slot in range(4 * STEPS):
            for at, size in tiles:
                here = pl.ds(at, size)
                wraps_of[slot, here] = pltpu.roll(edges[slot, group, here], turn, 1)

        def wrap(slot):
            return lambda here: wraps_of[slot, here]

        def row(c):
            return pl.multiple_of((c * count + p) * tall, 8)

        buffers = (state, later)
        for step in range(STEPS):
            now = buffers[step]
            last = step + 1 == STEPS

            def write_velocity(at, e_new, n_new):
                if not last:
                    later[1, pl.ds(at, 8)] = e_new
                    later[2, pl.ds(at, 8)] = n_new
                else:
                    grid_state[pl.ds(row(1) + (at - first), 8)] = e_new
                    grid_state[pl.ds(row(2) + (at - first), 8)] = n_new

            velocities(
                lambda c: now.at[c], coef, lambda c, here: wrap(4 * step + c)(here), write_velocity
            )

            def write_height(at, h_new):
                if not last:
                    later[0, pl.ds(at, 8)] = h_new
                else:
                    grid_state[pl.ds(row(0) + (at - first), 8)] = h_new

            heights(coef, wrap(4 * step + 3), write_height)
        return carry

    lax.fori_loop(0, count, body, 0)

    total[...] = jnp.zeros_like(total)

    def gram_body(i, acc):
        c, block = i // (rows // BLOCK), lax.rem(i, rows // BLOCK)
        at = c * count * tall + block * BLOCK + HALO
        values = jnp.concatenate(
            [grid_state[pl.ds(at + x, count, stride=tall)] for x in range(BLOCK)], 1
        )
        top = values.astype(jnp.bfloat16)
        low = (values - top.astype(jnp.float32)).astype(jnp.bfloat16)
        both = jnp.concatenate([top, low], 0)
        halves[i] = both
        return acc + lax.dot_general(
            both, both, (((1,), (1,)), ((), ())), preferred_element_type=jnp.float32
        )

    acc = jnp.zeros((2 * count, 2 * count), jnp.float32)
    acc = lax.fori_loop(0, fields * rows // BLOCK, gram_body, acc, unroll=4)
    total[:, : 2 * count] = acc
    value = total[...]
    summed = value[:count] + value[count:]
    summed = summed + pltpu.roll(summed, LANES - count, 1)
    lane = lane_ids(count)
    summed = jnp.where(lane < count, summed, 0.0)
    out = summed[:8]
    for b in range(1, count // 8):
        out = out + pltpu.roll(summed[8 * b : 8 * b + 8], count * b, 1)
    gram[...] = out


def evolve(probes, coefs, *received):
    fields, count, rows, cols = probes.shape
    tall = rows + 2 * TOP
    groups = count // 8
    f32 = jnp.float32
    return pl.pallas_call(
        evolve_kernel,
        out_shape=(
            jax.ShapeDtypeStruct((fields * rows // BLOCK, 2 * count, BLOCK * cols), jnp.bfloat16),
            jax.ShapeDtypeStruct((8, LANES), f32),
        ),
        scratch_shapes=[
            pltpu.VMEM((4, tall, LANES), f32),
            pltpu.VMEM((4, tall, LANES), f32),
            pltpu.VMEM((STEPS, fields, groups, tall, LANES), f32),
            pltpu.VMEM((4 * STEPS, groups, tall, LANES), f32),
            pltpu.VMEM((4 * STEPS, tall, LANES), f32),
            pltpu.VMEM((fields, tall, LANES), f32),
            pltpu.VMEM((fields, tall, LANES), f32),
            pltpu.VMEM((3, tall, LANES), f32),
            pltpu.VMEM((fields * count * (rows + 2 * HALO), LANES), f32),
            pltpu.VMEM((2 * count, LANES), f32),
        ],
        compiler_params=pltpu.CompilerParams(vmem_limit_bytes=VMEM_LIMIT),
        name="evolve_and_gram",
    )(probes, coefs, *received)


def finish_kernel(scale, grams, halves, basis, triangle, grid_out, staged, sems):
    fields, count, rows, cols = staged.shape
    stride = grid_out.shape[0] // count
    summed = jnp.sum(grams[...], 0)
    lane = lane_ids(count)
    row_id = lax.broadcasted_iota(jnp.int32, (count, LANES), 0)
    gram = jnp.concatenate(
        [summed if b == 0 else pltpu.roll(summed, LANES - count * b, 1) for b in range(count // 8)],
        0,
    )
    work = jnp.where(lane < count, gram, jnp.where(lane == row_id + count, 1.0, 0.0))
    for k in range(count):
        pivot_row = work[k : k + 1]
        ratio = work[:, k : k + 1] / work[k : k + 1, k : k + 1]
        work = work - jnp.where(row_id > k, ratio * pivot_row, 0.0)
    pivots = jnp.sum(jnp.where(lane == row_id, work, 0.0), 1, keepdims=True)
    work = work / jnp.sqrt(pivots)
    triangle[...] = jnp.where(lane >= row_id, work, 0.0)[:, :count] * (1.0 / scale)
    lower = (work * scale)[:, count : 2 * count]
    top = lower.astype(jnp.bfloat16)
    low = (lower - top.astype(jnp.float32)).astype(jnp.bfloat16)
    factor = jnp.concatenate([top, top, low], 1)

    copies = []
    for c in range(fields):

        def body(i, carry):
            both = halves[c * (rows // BLOCK) + i]
            stacked = jnp.concatenate([both, both[:count]], 0)
            out = jnp.dot(factor, stacked, preferred_element_type=jnp.float32)
            for x in range(BLOCK):
                at = BLOCK * i + x
                grid_out[pl.ds(at, count, stride=stride)] = out[:, x * cols : (x + 1) * cols]
            return carry

        lax.fori_loop(0, rows // BLOCK, body, 0, unroll=2)

        def store(q, carry):
            at = pl.multiple_of(q * stride, 8)
            staged[c, q] = grid_out[pl.ds(at, rows)].astype(jnp.bfloat16)
            return carry

        lax.fori_loop(0, count, store, 0, unroll=4)
        copies.append(pltpu.make_async_copy(staged.at[c], basis.at[c], sems.at[c]))
        copies[-1].start()
    for copy in copies:
        copy.wait()


def finish(grams, halves, shape, scale):
    fields, count, rows, cols = shape
    return pl.pallas_call(
        functools.partial(finish_kernel, scale),
        out_shape=(
            jax.ShapeDtypeStruct(shape, jnp.bfloat16),
            jax.ShapeDtypeStruct((count, count), jnp.float32),
        ),
        out_specs=(
            pl.BlockSpec(memory_space=pltpu.HBM),
            pl.BlockSpec(memory_space=pltpu.VMEM),
        ),
        scratch_shapes=[
            pltpu.VMEM((count * (rows + 8), cols), jnp.float32),
            pltpu.VMEM(shape, jnp.bfloat16),
            pltpu.SemaphoreType.DMA((fields,)),
        ],
        compiler_params=pltpu.CompilerParams(vmem_limit_bytes=VMEM_LIMIT),
        name="factor_and_apply",
    )(grams, halves)


def first_pairs(size):
    return [(i, i ^ 1) for i in range(size)]


def second_pairs(size):
    return [(i, ((i + 1) ^ 1) - 1) for i in range(1, size - 1)]


def per_device(probes, depth, east_flow, north_flow, land_sea):
    fields, count, rows, cols = probes.shape
    nx, ny = lax.axis_size("gx"), lax.axis_size("gy")
    even_x = lax.rem(lax.axis_index("gx"), 2) == 0
    x_a, x_b, to_a, to_b, held, coefs = pack(probes, depth, east_flow, north_flow, land_sea)
    from_b = lax.ppermute(to_b, "gy", second_pairs(ny))
    from_a = lax.ppermute(to_a, "gy", first_pairs(ny))
    got_xb = lax.ppermute(x_b, "gx", second_pairs(nx))
    got_xa = lax.ppermute(x_a, "gx", first_pairs(nx))
    even_y = lax.rem(lax.axis_index("gy"), 2) == 0
    rows_of = (
        jnp.where(even_y, from_b, from_a),
        jnp.where(even_y, to_b, to_a),
        jnp.where(even_y, to_a, to_b),
        jnp.where(even_y, from_a, from_b),
    )
    low = jnp.stack([k[:, :HALO] for k in rows_of])
    high = jnp.stack([k[:, rows - HALO :] for k in rows_of])
    c_b = lax.ppermute(jnp.where(even_x, low, high), "gx", second_pairs(nx))
    c_a = lax.ppermute(jnp.where(even_x, high, low), "gx", first_pairs(nx))
    halves, gram = evolve(held, coefs, got_xa, got_xb, to_a, to_b, from_a, from_b, c_a, c_b)
    devices = nx * ny
    grams = lax.all_to_all(
        jnp.broadcast_to(gram[None], (devices,) + gram.shape), ("gx", "gy"), 0, 0
    )
    scale = math.sqrt(fields * rows * nx * cols * ny)
    return finish(grams, halves, probes.shape, scale)


def solution(mesh):
    in_specs = (
        P(None, None, "gx", "gy"),
        P("gx", "gy"),
        P("gx", "gy"),
        P("gx", "gy"),
        P("gx", "gy"),
    )
    out_specs = (P(None, None, "gx", "gy"), P())
    return jax.shard_map(
        per_device, mesh=mesh, in_specs=in_specs, out_specs=out_specs, check_vma=False
    )
```

time: 150 us -> 71.3 us (0.48)
  Pallas kernels: 111 us -> 34 us
  local copies, waits for them, and re-layouts: 2.1 us -> 6.48 us
  starting transfers between devices: 15.1 us -> 10.8 us
  waiting for transfers between devices: 4.49 us -> 1.9 us
    pallas_call x1, Pallas kernels: 89 us -> 23.3 us  [evolve(): pl.pallas_call(evolve_kernel, out_shape=(jax.ShapeDtypeStruct((fields * r...]
    pallas_call x1, Pallas kernels: 10.5 us -> 2.64 us  [pack(): pl.pallas_call(pack_kernel, in_specs=[pl.BlockSpec(memory_space=pltpu.HBM...]
    unnamed x12 -> x14, local copies, waits for them, and re-layouts: 0.61 us -> 6.45 us
    ppermute x6, starting transfers between devices: 15.1 us -> 10.8 us  [the longest x1 5.71 us: per_device(): c_a = lax.ppermute(jnp.where(even_x, high, low), 'gx', first_pairs(nx))]
    pallas_call x1, Pallas kernels: 11.8 us -> 8.08 us  [finish(): pl.pallas_call(functools.partial(finish_kernel, scale), out_shape=(jax.Sh...]
    ppermute x6, waiting for transfers between devices: 4.49 us -> 1.9 us  [the longest x1 1.88 us: per_device(): c_a = lax.ppermute(jnp.where(even_x, high, low), 'gx', first_pairs(nx))]
  transfers between devices with their start and end apart: 6 -> 6, of which waited for: 2 -> 1; matrix products, arithmetic and copies ran while one was open for 1% -> 0% of each run, Pallas kernels for 0% -> 0%
where the time goes in v1:
time: 71.3 us; the launch traced here: 70.8 us
  Pallas kernels  34 us (48%)
  blocking collectives  16.8 us (24%)
  starting transfers between devices  10.8 us (15%)
  local copies, waits for them, and re-layouts  6.48 us (9%)
  waiting for transfers between devices  1.9 us (3%)
  between operations  0.77 us (1%)
    pallas_call x1, Pallas kernels, evolve(): pl.pallas_call(evolve_kernel, out_shape=(jax.ShapeDtypeStruct((fields * r...  23.3 us
    all_to_all x1, blocking collectives, per_device(): lax.all_to_all(jnp.broadcast_to(gram[None], (devices,) + gram.shape), ('g...  16.8 us
    pallas_call x1, Pallas kernels, finish(): pl.pallas_call(functools.partial(finish_kernel, scale), out_shape=(jax.Sh...  8.08 us
    unnamed x14, local copies, waits for them, and re-layouts  6.45 us
    ppermute x1, starting transfers between devices, per_device(): c_a = lax.ppermute(jnp.where(even_x, high, low), 'gx', first_pairs(nx))  5.71 us
    pallas_call x1, Pallas kernels, pack(): pl.pallas_call(pack_kernel, in_specs=[pl.BlockSpec(memory_space=pltpu.HBM...  2.64 us
    ppermute x1, starting transfers between devices, per_device(): got_xa = lax.ppermute(x_a, 'gx', first_pairs(nx))  2.64 us
    ppermute x1, waiting for transfers between devices, per_device(): c_a = lax.ppermute(jnp.where(even_x, high, low), 'gx', first_pairs(nx))  1.88 us
  transfers between devices with their start and end apart: 6, of which 1 were waited for; matrix products, arithmetic and copies ran while one was open for 0% of the time, Pallas kernels for 0%

profile of v1, /device:TPU:0, one launch (start us, length us, event | category | flops | bytes accessed | tf_op | source)
XLA Modules:
  0.0 70.8 jit_solution(10442759034744406225)
XLA Ops:
  0.6 0.0 copy-start
  0.6 1.7 %copy-done = bf16[3,32,96,128]{3,2,1,0:T(8,128)(2,1)S(1)} copy-done((bf16[3,32,96,128]{3,2,1,0:T(8,128)(2,1)S(1)}, bf16[3,32,96,128]{3,2,1,0:T(8,128)(2,1)}, u32[]{:S(2)}) %copy-start) | copy-done | bytes 2359320
  2.3 0.0 copy-start.3
  2.3 0.8 %copy-done.3 = f32[96,128]{1,0:T(8,128)S(1)} copy-done((f32[96,128]{1,0:T(8,128)S(1)}, f32[96,128]{1,0:T(8,128)}, u32[]{:S(2)}) %copy-start.3) | copy-done | bytes 49176
  3.1 0.0 copy-start.4
  3.1 0.8 %copy-done.4 = f32[96,128]{1,0:T(8,128)S(1)} copy-done((f32[96,128]{1,0:T(8,128)S(1)}, f32[96,128]{1,0:T(8,128)}, u32[]{:S(2)}) %copy-start.4) | copy-done | bytes 49176
  3.9 0.0 copy-start.5
  3.9 0.8 %copy-done.5 = f32[96,128]{1,0:T(8,128)S(1)} copy-done((f32[96,128]{1,0:T(8,128)S(1)}, f32[96,128]{1,0:T(8,128)}, u32[]{:S(2)}) %copy-start.5) | copy-done | bytes 49176
  4.7 0.0 copy-start.6
  4.7 0.8 %copy-done.6 = s32[96,128]{1,0:T(8,128)S(1)} copy-done((s32[96,128]{1,0:T(8,128)S(1)}, s32[96,128]{1,0:T(8,128)}, u32[]{:S(2)}) %copy-start.6) | copy-done | bytes 49176
  5.5 2.6 %pack_edges.1 = (f32[100,4,128]{2,1,0:T(4,128)}, f32[100,4,128]{2,1,0:T(4,128)}, f32[4,96,128]{2,1,0:T(8,128)S(1)}, f32[4,96,128]{2,1,0:T(8,128)S(1)}, bf16[3,32...) custom-call(bf16[3,32,96,128]{3,2,1,0:T(8,128)(2,1)S(1)} %copy-done, f32[96,128]{1,0:T(8,128)S(1)} %copy-done.3, ...), custom_call_target="tpu_custom_call" | custom-call | tf_op jit(solution)/shard_map/pack_edges/pallas_call | solution.py:90
  8.1 0.0 copy-start.1
  8.2 0.7 copy-done.1
  8.8 0.5 collective-permute-start.2
  9.3 0.7 collective-permute-start.3
  9.9 2.6 %collective-permute-start = (f32[100,4,128]{2,1,0:T(4,128)}, f32[100,4,128]{2,1,0:T(4,128)S(1)}, u32[]{:S(2)}, u32[]{:S(2)}) collective-permute-start(f32[100,4,128]{2,1,0:T(4,128)} %get-tuple-element.12), channel_id=1, source_target_pairs={{0,8},{8,0},{16,24},{24,16},{1,9},{9,1},{17,25},{25,17},{2,10},{10... | collective-permute-start | bytes 614408 | tf_op jit(solution)/shard_map/ppermute | solution.py:428
  12.6 0.7 collective-permute-start.1
  13.3 0.0 collective-permute-done.2.from_a
  13.3 0.0 collective-permute-done.3.from_b
  13.4 0.7 collective-permute-start.5
  14.1 5.7 %collective-permute-start.4 = (f32[4,4,4,128]{3,2,1,0:T(4,128)S(1)}, f32[4,4,4,128]{3,2,1,0:T(4,128)S(1)}, u32[]{:S(2)}, u32[]{:S(2)}) collective-permute-start(f32[4,4,4,128]{3,2,1,0:T(4,128)S(1)} %get-tuple-element.31), channel_id=1, source_target_pairs={{0,8},{8,0},{16,24},{24,16},{1,9},{9,1},{17,25},{25,17},{2,10},{10... | collective-permute-start | bytes 98312 | tf_op jit(solution)/shard_map/ppermute | solution.py:439
  19.8 0.0 collective-permute-done.x_a
  19.8 0.0 collective-permute-done.1.x_b
  19.8 0.0 collective-permute-done.5.c_b
  19.8 1.9 %collective-permute-done.4.c_a = f32[4,4,4,128]{3,2,1,0:T(4,128)S(1)} collective-permute-done((f32[4,4,4,128]{3,2,1,0:T(4,128)S(1)}, f32[4,4,4,128]{3,2,1,0:T(4,128)S(1)}, u32[]{:S(2)}, u32[]{:S(2)}) %collective-permute-start.4) | collective-permute-done | bytes 32800 | tf_op jit(solution)/shard_map/ppermute | solution.py:439
  21.7 0.0 copy-start.2
  21.7 0.9 %copy-done.2 = f32[4,96,128]{2,1,0:T(8,128)S(1)} copy-done((f32[4,96,128]{2,1,0:T(8,128)S(1)}, f32[4,96,128]{2,1,0:T(8,128)}, u32[]{:S(2)}) %copy-start.2) | copy-done | bytes 196632
  22.6 23.3 %evolve_and_gram.1 = (bf16[36,64,1024]{2,1,0:T(8,128)(2,1)S(1)}, f32[8,128]{1,0:T(8,128)S(1)}) custom-call(bf16[3,32,96,128]{3,2,1,0:T(8,128)(2,1)S(1)} %get-tuple-element.10.probes, f32[4,96,128]{2,1,0:T(8,128)S(1)} %copy-done.2, f32[100,4,128]{2,1,0:T(4,128)S(1)} %collective-permute-done.x_a, f32[100,4,128]{2,1,0:T(4,128)S(1)} %collective-permute-done.1.x_b, ...), custom_call_target="tpu_custom_call" | custom-call | tf_op jit(solution)/shard_map/evolve_and_gram/pallas_call | solution.py:318
  45.9 16.8 %all_to_all.5.grams = f32[32,8,128]{2,1,0:T(8,128)S(1)} all-to-all(f32[32,8,128]{2,1,0:T(8,128)S(1)} %broadcast_in_dim.2), channel_id=1, replica_groups=mesh['gx'=4,'gy'=8] {'gx','gy'}, dimensions={0} | all-to-all | bytes 262144 | tf_op jit(solution)/shard_map/all_to_all | solution.py:442
  62.7 8.1 %factor_and_apply.1 = (bf16[3,32,96,128]{3,2,1,0:T(8,128)(2,1)}, f32[32,32]{1,0:T(8,128)}) custom-call(f32[32,8,128]{2,1,0:T(8,128)S(1)} %all_to_all.5.grams, bf16[36,64,1024]{2,1,0:T(8,128)(2,1)S(1)} %get-tuple-element.17.halves), custom_call_target="tpu_custom_call" | custom-call | tf_op jit(solution)/shard_map/factor_and_apply/pallas_call | solution.py:392
  (6 shorter events, 0.1 us)
Async XLA Ops:
  0.6 1.7 %copy-start = (bf16[3,32,96,128]{3,2,1,0:T(8,128)(2,1)S(1)}, bf16[3,32,96,128]{3,2,1,0:T(8,128)(2,1)}, u32[]{:S(2)}) copy-start(bf16[3,32,96,128]{3,2,1,0:T(8,128)(2,1)} %probes.1) | copy-start | bytes 7077892
  2.3 0.8 %copy-start.3 = (f32[96,128]{1,0:T(8,128)S(1)}, f32[96,128]{1,0:T(8,128)}, u32[]{:S(2)}) copy-start(f32[96,128]{1,0:T(8,128)} %depth.1) | copy-start | bytes 147460
  3.1 0.8 %copy-start.4 = (f32[96,128]{1,0:T(8,128)S(1)}, f32[96,128]{1,0:T(8,128)}, u32[]{:S(2)}) copy-start(f32[96,128]{1,0:T(8,128)} %east_flow.1) | copy-start | bytes 147460
  3.9 0.8 %copy-start.5 = (f32[96,128]{1,0:T(8,128)S(1)}, f32[96,128]{1,0:T(8,128)}, u32[]{:S(2)}) copy-start(f32[96,128]{1,0:T(8,128)} %north_flow.1) | copy-start | bytes 147460
  4.7 0.8 %copy-start.6 = (s32[96,128]{1,0:T(8,128)S(1)}, s32[96,128]{1,0:T(8,128)}, u32[]{:S(2)}) copy-start(s32[96,128]{1,0:T(8,128)} %land_sea.1) | copy-start | bytes 147460
  8.1 0.7 copy-start.1
  8.8 4.5 %collective-permute-start.2 = (f32[4,96,128]{2,1,0:T(8,128)S(1)}, f32[4,96,128]{2,1,0:T(8,128)S(1)}, u32[]{:S(2)}, u32[]{:S(2)}) collective-permute-start(f32[4,96,128]{2,1,0:T(8,128)S(1)} %get-tuple-element.14.to_a), channel_id=1, source_target_pairs={{0,1},{1,0},{2,3},{3,2},{4,5},{5,4},{6,7},{7,6},{8,9},{9,8},{10,11... | collective-permute-start | bytes 589832 | tf_op jit(solution)/shard_map/ppermute | solution.py:426
  9.3 4.1 %collective-permute-start.3 = (f32[4,96,128]{2,1,0:T(8,128)S(1)}, f32[4,96,128]{2,1,0:T(8,128)S(1)}, u32[]{:S(2)}, u32[]{:S(2)}) collective-permute-start(f32[4,96,128]{2,1,0:T(8,128)S(1)} %get-tuple-element.15.to_b), channel_id=1, source_target_pairs={{1,2},{2,1},{3,4},{4,3},{5,6},{6,5},{9,10},{10,9},{11,12},{12,11},... | collective-permute-start | bytes 589832 | tf_op jit(solution)/shard_map/ppermute | solution.py:425
  9.9 9.9 %collective-permute-start = (f32[100,4,128]{2,1,0:T(4,128)}, f32[100,4,128]{2,1,0:T(4,128)S(1)}, u32[]{:S(2)}, u32[]{:S(2)}) collective-permute-start(f32[100,4,128]{2,1,0:T(4,128)} %get-tuple-element.12), channel_id=1, source_target_pairs={{0,8},{8,0},{16,24},{24,16},{1,9},{9,1},{17,25},{25,17},{2,10},{10... | collective-permute-start | bytes 614408 | tf_op jit(solution)/shard_map/ppermute | solution.py:428
  12.6 7.2 %collective-permute-start.1 = (f32[100,4,128]{2,1,0:T(4,128)}, f32[100,4,128]{2,1,0:T(4,128)S(1)}, u32[]{:S(2)}, u32[]{:S(2)}) collective-permute-start(f32[100,4,128]{2,1,0:T(4,128)} %get-tuple-element.13), channel_id=1, source_target_pairs={{8,16},{16,8},{9,17},{17,9},{10,18},{18,10},{11,19},{19,11},{12,20... | collective-permute-start | bytes 614408 | tf_op jit(solution)/shard_map/ppermute | solution.py:427
  13.4 6.4 %collective-permute-start.5 = (f32[4,4,4,128]{3,2,1,0:T(4,128)S(1)}, f32[4,4,4,128]{3,2,1,0:T(4,128)S(1)}, u32[]{:S(2)}, u32[]{:S(2)}) collective-permute-start(f32[4,4,4,128]{3,2,1,0:T(4,128)S(1)} %get-tuple-element.30), channel_id=1, source_target_pairs={{8,16},{16,8},{9,17},{17,9},{10,18},{18,10},{11,19},{19,11},{12,20... | collective-permute-start | bytes 98312 | tf_op jit(solution)/shard_map/ppermute | solution.py:438
  14.1 7.6 %collective-permute-start.4 = (f32[4,4,4,128]{3,2,1,0:T(4,128)S(1)}, f32[4,4,4,128]{3,2,1,0:T(4,128)S(1)}, u32[]{:S(2)}, u32[]{:S(2)}) collective-permute-start(f32[4,4,4,128]{3,2,1,0:T(4,128)S(1)} %get-tuple-element.31), channel_id=1, source_target_pairs={{0,8},{8,0},{16,24},{24,16},{1,9},{9,1},{17,25},{25,17},{2,10},{10... | collective-permute-start | bytes 98312 | tf_op jit(solution)/shard_map/ppermute | solution.py:439
  21.7 0.9 %copy-start.2 = (f32[4,96,128]{2,1,0:T(8,128)S(1)}, f32[4,96,128]{2,1,0:T(8,128)}, u32[]{:S(2)}) copy-start(f32[4,96,128]{2,1,0:T(8,128)} %copy-done.1) | copy-start | bytes 589828

commit v2 on v1

--- a/solution.py
+++ b/solution.py
@@ -19,6 +19,8 @@
 
 VMEM_LIMIT = 24 * 1024 * 1024
 BLOCK = 8
+JOIN = 1
+WIDE = 4
 
 
 def lane_ids(rows):
@@ -82,7 +84,8 @@
         columns_out(c, low, high)
 
 
-def pack(probes, depth, east_flow, north_flow, land_sea):
+def pack(*arguments):
+    probes = arguments[0]
     fields, count, rows, cols = probes.shape
     f32 = jnp.float32
     x_shape = jax.ShapeDtypeStruct((fields * count + 4, HALO, cols), f32)
@@ -101,12 +104,13 @@
         ],
         compiler_params=pltpu.CompilerParams(vmem_limit_bytes=VMEM_LIMIT),
         name="pack_edges",
-    )(probes, depth, east_flow, north_flow, land_sea)
+    )(*[pltpu.with_memory_space_constraint(v, pltpu.HBM) for v in arguments])
 
 
 def evolve_kernel(
     probes, coefs, x_a, x_b, to_a, to_b, from_a, from_b, c_a, c_b,
-    halves, gram, coef, strip_coef, strips, edges, wraps_of, state, later, flux, grid_state, total,
+    halves, gram, coef, strip_coef, strips, edges, weights,
+    wraps_of, state, later, flux, slope, grid_state, total,
 ):
     fields, count, rows, _ = probes.shape
     own = pl.ds(TOP, rows)
@@ -114,6 +118,8 @@
     tall = rows + 2 * HALO
     first = TOP - HALO
     tiles = [(first + 8 * t, 8) for t in range(tall // 8)]
+    padded = 16 * ((tall + 15) // 16)
+    window = pl.ds(first, padded)
     lane8 = lane_ids(8)
     half = 0.5 * time_step
     even_x = lax.rem(lax.axis_index("gx"), 2) == 0
@@ -175,6 +181,16 @@
     unpack(0, 8, lambda k, c: jnp.concatenate([whole, jnp.where(even_x, c_b[k, c], c_a[k, c])], 0))
     unpack(bottom, 8, lambda k, c: jnp.concatenate([jnp.where(even_x, c_a[k, c], c_b[k, c]), whole], 0))
 
+    source = lax.broadcasted_iota(jnp.int32, (2 * LANES, LANES), 0) & (LANES - 1)
+    target = lax.broadcasted_iota(jnp.int32, (2 * LANES, LANES), 1)
+    weights[...] = (
+        (source == target + 1).astype(jnp.float32) - (source == target - 1).astype(jnp.float32)
+    ).astype(jnp.bfloat16)
+
+    def two(value):
+        top = value.astype(jnp.bfloat16)
+        return top, (value - top.astype(jnp.float32)).astype(jnp.bfloat16)
+
     def shifted(value, wrap):
         if wrap is None:
             return pltpu.roll(value, LANES - 1, 1) - pltpu.roll(value, 1, 1)
@@ -182,13 +198,13 @@
         down = jnp.where(lane8 == LANES - 1, wrap, value)
         return pltpu.roll(up, LANES - 1, 1) - pltpu.roll(down, 1, 1)
 
-    def velocities(source, factors, wraps, write):
+    def velocities(source, factors, differences, flux, write):
         for at, size in tiles:
             here, above, below = pl.ds(at, size), pl.ds(at - 1, size), pl.ds(at + 1, size)
             deep, east, north, slope = [factors[a, here] for a in range(4)]
             h, e, n = [source(c)[here] for c in range(3)]
             xh, xe, xn = [source(c)[below] - source(c)[above] for c in range(3)]
-            yh, ye, yn = [shifted(v, wraps(c, here)) for c, v in enumerate((h, e, n))]
+            yh, ye, yn = [differences(c, at, v) for c, v in enumerate((h, e, n))]
             e_new = e + (time_step * coriolis) * n - (east * xe + north * ye + slope * xh)
             n_new = n - (time_step * coriolis) * e - (east * xn + north * yn + slope * yh)
             write(at, e_new, n_new)
@@ -196,11 +212,11 @@
             flux[1, here] = deep * n_new
             flux[2, here] = h - (east * xh + north * yh)
 
-    def heights(factors, wraps, write):
+    def heights(factors, differences, flux, write):
         for at, size in tiles:
             here, above, below = pl.ds(at, size), pl.ds(at - 1, size), pl.ds(at + 1, size)
             along = flux[0, below] - flux[0, above]
-            across = shifted(flux[1, here], wraps(here))
+            across = differences(at)
             write(at, flux[2, here] - factors[3, here] * (along + across))
 
     def keep(slot, g, at, size, value):
@@ -209,6 +225,7 @@
         )
 
     def strip_body(g, carry):
+        mine = flux.at[0]
         for step in range(STEPS):
             for at, size in tiles:
                 for c in range(fields):
@@ -220,65 +237,93 @@
                     strips[step + 1, 2, g, pl.ds(at, 8)] = n_new
 
             velocities(
-                lambda c: strips.at[step, c, g], strip_coef, lambda c, here: None, write_velocity
+                lambda c: strips.at[step, c, g], strip_coef,
+                lambda c, at, value: shifted(value, None), mine, write_velocity,
             )
             for at, size in tiles:
-                keep(4 * step + 3, g, at, size, flux[1, pl.ds(at, size)])
+                value = mine[1, pl.ds(at, size)]
+                part = lax.rem(lane8, 16)
+                edges[4 * step + 3, g, pl.ds(at, size)] = jnp.where(
+                    part == HALO, -pltpu.roll(value, 1, 1), pltpu.roll(value, LANES - 9, 1)
+                )
             if step + 1 < STEPS:
 
                 def write_height(at, h_new):
                     strips[step + 1, 0, g, pl.ds(at, 8)] = h_new
 
-                heights(strip_coef, lambda here: None, write_height)
+                heights(
+                    strip_coef, lambda at: shifted(mine[1, pl.ds(at, 8)], None), mine, write_height
+                )
         return carry
 
     lax.fori_loop(0, groups, strip_body, 0)
 
-    def body(p, carry):
-        group = p // 8
-        turn = lax.rem(2 * LANES - 16 * lax.rem(p, 8) - HALO, LANES)
-        for c in range(fields):
-            state[c, own] = probes[c, p].astype(jnp.float32) * coefs[3]
-            state[c, pl.ds(first, HALO)] = x_before(c * count + p)
-            state[c, pl.ds(bottom, HALO)] = x_after(c * count + p)
-        for slot in range(4 * STEPS):
-            for at, size in tiles:
-                here = pl.ds(at, size)
-                wraps_of[slot, here] = pltpu.roll(edges[slot, group, here], turn, 1)
-
-        def wrap(slot):
-            return lambda here: wraps_of[slot, here]
-
-        def row(c):
-            return pl.multiple_of((c * count + p) * tall, 8)
-
-        buffers = (state, later)
+    ends = (lane8 == 0) | (lane8 == LANES - 1)
+
+    def body(i, carry):
+        def begin(k):
+            p = WIDE * i + k
+            group, slot = p // 8, lax.rem(p, 8)
+            turn = lax.rem(2 * LANES - 16 * slot - HALO, LANES)
+            for c in range(fields):
+                state[k, c, own] = probes[c, p].astype(jnp.float32) * coefs[3]
+                state[k, c, pl.ds(first, HALO)] = x_before(c * count + p)
+                state[k, c, pl.ds(bottom, HALO)] = x_after(c * count + p)
+            for slot in range(4 * STEPS):
+                for at, size in tiles:
+                    here = pl.ds(at, size)
+                    wraps_of[k, slot, here] = pltpu.roll(edges[slot, group, here], turn, 1)
+
+        for k in range(WIDE):
+            begin(k)
+
         for step in range(STEPS):
-            now = buffers[step]
             last = step + 1 == STEPS
-
-            def write_velocity(at, e_new, n_new):
-                if not last:
-                    later[1, pl.ds(at, 8)] = e_new
-                    later[2, pl.ds(at, 8)] = n_new
-                else:
-                    grid_state[pl.ds(row(1) + (at - first), 8)] = e_new
-                    grid_state[pl.ds(row(2) + (at - first), 8)] = n_new
-
-            velocities(
-                lambda c: now.at[c], coef, lambda c, here: wrap(4 * step + c)(here), write_velocity
-            )
-
-            def write_height(at, h_new):
-                if not last:
-                    later[0, pl.ds(at, 8)] = h_new
-                else:
-                    grid_state[pl.ds(row(0) + (at - first), 8)] = h_new
-
-            heights(coef, wrap(4 * step + 3), write_height)
+            for k in range(WIDE):
+
+                def row(c):
+                    return pl.multiple_of((c * count + WIDE * i + k) * tall, 8)
+
+                def write_velocity(at, e_new, n_new):
+                    if not last:
+                        later[k, 1, pl.ds(at, 8)] = e_new
+                        later[k, 2, pl.ds(at, 8)] = n_new
+                    else:
+                        grid_state[pl.ds(row(1) + (at - first), 8)] = e_new
+                        grid_state[pl.ds(row(2) + (at - first), 8)] = n_new
+
+                now = (state, later)[step]
+                velocities(
+                    lambda c: now.at[k, c], coef,
+                    lambda c, at, value: shifted(value, wraps_of[k, 4 * step + c, pl.ds(at, 8)]),
+                    flux.at[k], write_velocity,
+                )
+            for j in range(0, WIDE, JOIN):
+                left = jnp.concatenate(
+                    [jnp.concatenate(two(flux[k, 1, window]), 1) for k in range(j, j + JOIN)], 0
+                )
+                slope[j * padded : (j + JOIN) * padded] = jnp.dot(
+                    left, weights[...], preferred_element_type=jnp.float32
+                )
+            for k in range(WIDE):
+
+                def row(c):
+                    return pl.multiple_of((c * count + WIDE * i + k) * tall, 8)
+
+                def write_height(at, h_new):
+                    if not last:
+                        later[k, 0, pl.ds(at, 8)] = h_new
+                    else:
+                        grid_state[pl.ds(row(0) + (at - first), 8)] = h_new
+
+                def across(at):
+                    wrap = wraps_of[k, 4 * step + 3, pl.ds(at, 8)]
+                    return slope[pl.ds(k * padded + at - first, 8)] + jnp.where(ends, wrap, 0.0)
+
+                heights(coef, across, flux.at[k], write_height)
         return carry
 
-    lax.fori_loop(0, count, body, 0)
+    lax.fori_loop(0, count // WIDE, body, 0)
 
     total[...] = jnp.zeros_like(total)
 
@@ -312,7 +357,8 @@
 
 def evolve(probes, coefs, *received):
     fields, count, rows, cols = probes.shape
-    tall = rows + 2 * TOP
+    padded = 16 * ((rows + 2 * HALO + 15) // 16)
+    tall = padded + TOP
     groups = count // 8
     f32 = jnp.float32
     return pl.pallas_call(
@@ -326,10 +372,12 @@
             pltpu.VMEM((4, tall, LANES), f32),
             pltpu.VMEM((STEPS, fields, groups, tall, LANES), f32),
             pltpu.VMEM((4 * STEPS, groups, tall, LANES), f32),
-            pltpu.VMEM((4 * STEPS, tall, LANES), f32),
-            pltpu.VMEM((fields, tall, LANES), f32),
-            pltpu.VMEM((fields, tall, LANES), f32),
-            pltpu.VMEM((3, tall, LANES), f32),
+            pltpu.VMEM((2 * LANES, LANES), jnp.bfloat16),
+            pltpu.VMEM((WIDE, 4 * STEPS, tall, LANES), f32),
+            pltpu.VMEM((WIDE, fields, tall, LANES), f32),
+            pltpu.VMEM((WIDE, fields, tall, LANES), f32),
+            pltpu.VMEM((WIDE, 3, tall, LANES), f32),
+            pltpu.VMEM((WIDE * padded, LANES), f32),
             pltpu.VMEM((fields * count * (rows + 2 * HALO), LANES), f32),
             pltpu.VMEM((2 * count, LANES), f32),
         ],

time: 71.3 us -> 61.4 us (0.86)
  local copies, waits for them, and re-layouts: 6.48 us -> 1.63 us
  Pallas kernels: 34 us -> 29.2 us
    pallas_call x1, Pallas kernels: 23.3 us -> 17.7 us  [evolve(): pl.pallas_call(evolve_kernel, out_shape=(jax.ShapeDtypeStruct((fields * r...]
    unnamed x14 -> x4, local copies, waits for them, and re-layouts: 6.45 us -> 1.59 us
    pallas_call x1, Pallas kernels: 2.64 us -> 3.41 us  [pack(): pl.pallas_call(pack_kernel, in_specs=[pl.BlockSpec(memory_space=pltpu.HBM...]
where the time goes in v2:
time: 61.4 us; the launch traced here: 61.1 us
  Pallas kernels  29.2 us (48%)
  blocking collectives  16.8 us (27%)
  starting transfers between devices  10.8 us (18%)
  waiting for transfers between devices  1.9 us (3%)
  local copies, waits for them, and re-layouts  1.63 us (3%)
  between operations  0.75 us (1%)
    pallas_call x1, Pallas kernels, evolve(): pl.pallas_call(evolve_kernel, out_shape=(jax.ShapeDtypeStruct((fields * r...  17.7 us
    all_to_all x1, blocking collectives, per_device(): lax.all_to_all(jnp.broadcast_to(gram[None], (devices,) + gram.shape), ('g...  16.8 us
    pallas_call x1, Pallas kernels, finish(): pl.pallas_call(functools.partial(finish_kernel, scale), out_shape=(jax.Sh...  8.09 us
    ppermute x1, starting transfers between devices, per_device(): c_a = lax.ppermute(jnp.where(even_x, high, low), 'gx', first_pairs(nx))  5.71 us
    pallas_call x1, Pallas kernels, pack(): pl.pallas_call(pack_kernel, in_specs=[pl.BlockSpec(memory_space=pltpu.HBM...  3.41 us
    ppermute x1, starting transfers between devices, per_device(): got_xa = lax.ppermute(x_a, 'gx', first_pairs(nx))  2.64 us
    ppermute x1, waiting for transfers between devices, per_device(): c_a = lax.ppermute(jnp.where(even_x, high, low), 'gx', first_pairs(nx))  1.88 us
    unnamed x4, local copies, waits for them, and re-layouts  1.59 us
  transfers between devices with their start and end apart: 6, of which 1 were waited for; matrix products, arithmetic and copies ran while one was open for 0% of the time, Pallas kernels for 0%

profile of v2, /device:TPU:0, one launch (start us, length us, event | category | flops | bytes accessed | tf_op | source)
XLA Modules:
  0.0 61.1 jit_solution(11356813557265210837)
XLA Ops:
  0.6 3.4 %pack_edges.1 = (f32[100,4,128]{2,1,0:T(4,128)}, f32[100,4,128]{2,1,0:T(4,128)}, f32[4,96,128]{2,1,0:T(8,128)S(1)}, f32[4,96,128]{2,1,0:T(8,128)S(1)}, bf16[3,32...) custom-call(bf16[3,32,96,128]{3,2,1,0:T(8,128)(2,1)} %probes.1, f32[96,128]{1,0:T(8,128)} %depth.1, ...), custom_call_target="tpu_custom_call" | custom-call | tf_op jit(solution)/shard_map/pack_edges/pallas_call | solution.py:93
  4.0 0.0 copy-start
  4.1 0.7 %copy-done = f32[4,96,128]{2,1,0:T(8,128)} copy-done((f32[4,96,128]{2,1,0:T(8,128)}, f32[4,96,128]{2,1,0:T(8,128)S(1)}, u32[]{:S(2)}) %copy-start) | copy-done | bytes 196632
  4.7 0.5 collective-permute-start.2
  5.2 0.7 %collective-permute-start.3 = (f32[4,96,128]{2,1,0:T(8,128)S(1)}, f32[4,96,128]{2,1,0:T(8,128)S(1)}, u32[]{:S(2)}, u32[]{:S(2)}) collective-permute-start(f32[4,96,128]{2,1,0:T(8,128)S(1)} %get-tuple-element.15.to_b), channel_id=1, source_target_pairs={{1,2},{2,1},{3,4},{4,3},{5,6},{6,5},{9,10},{10,9},{11,12},{12,11},... | collective-permute-start | bytes 589832 | tf_op jit(solution)/shard_map/ppermute | solution.py:473
  5.8 2.6 %collective-permute-start = (f32[100,4,128]{2,1,0:T(4,128)}, f32[100,4,128]{2,1,0:T(4,128)S(1)}, u32[]{:S(2)}, u32[]{:S(2)}) collective-permute-start(f32[100,4,128]{2,1,0:T(4,128)} %get-tuple-element.12), channel_id=1, source_target_pairs={{0,8},{8,0},{16,24},{24,16},{1,9},{9,1},{17,25},{25,17},{2,10},{10... | collective-permute-start | bytes 614408 | tf_op jit(solution)/shard_map/ppermute | solution.py:476
  8.5 0.7 %collective-permute-start.1 = (f32[100,4,128]{2,1,0:T(4,128)}, f32[100,4,128]{2,1,0:T(4,128)S(1)}, u32[]{:S(2)}, u32[]{:S(2)}) collective-permute-start(f32[100,4,128]{2,1,0:T(4,128)} %get-tuple-element.13), channel_id=1, source_target_pairs={{8,16},{16,8},{9,17},{17,9},{10,18},{18,10},{11,19},{19,11},{12,20... | collective-permute-start | bytes 614408 | tf_op jit(solution)/shard_map/ppermute | solution.py:475
  9.2 0.0 collective-permute-done.2.from_a
  9.2 0.0 collective-permute-done.3.from_b
  9.3 0.7 %collective-permute-start.5 = (f32[4,4,4,128]{3,2,1,0:T(4,128)S(1)}, f32[4,4,4,128]{3,2,1,0:T(4,128)S(1)}, u32[]{:S(2)}, u32[]{:S(2)}) collective-permute-start(f32[4,4,4,128]{3,2,1,0:T(4,128)S(1)} %get-tuple-element.30), channel_id=1, source_target_pairs={{8,16},{16,8},{9,17},{17,9},{10,18},{18,10},{11,19},{19,11},{12,20... | collective-permute-start | bytes 98312 | tf_op jit(solution)/shard_map/ppermute | solution.py:486
  10.0 5.7 %collective-permute-start.4 = (f32[4,4,4,128]{3,2,1,0:T(4,128)S(1)}, f32[4,4,4,128]{3,2,1,0:T(4,128)S(1)}, u32[]{:S(2)}, u32[]{:S(2)}) collective-permute-start(f32[4,4,4,128]{3,2,1,0:T(4,128)S(1)} %get-tuple-element.31), channel_id=1, source_target_pairs={{0,8},{8,0},{16,24},{24,16},{1,9},{9,1},{17,25},{25,17},{2,10},{10... | collective-permute-start | bytes 98312 | tf_op jit(solution)/shard_map/ppermute | solution.py:487
  15.7 0.0 collective-permute-done.x_a
  15.7 0.0 collective-permute-done.1.x_b
  15.7 0.0 collective-permute-done.5.c_b
  15.7 1.9 %collective-permute-done.4.c_a = f32[4,4,4,128]{3,2,1,0:T(4,128)S(1)} collective-permute-done((f32[4,4,4,128]{3,2,1,0:T(4,128)S(1)}, f32[4,4,4,128]{3,2,1,0:T(4,128)S(1)}, u32[]{:S(2)}, u32[]{:S(2)}) %collective-permute-start.4) | collective-permute-done | bytes 32800 | tf_op jit(solution)/shard_map/ppermute | solution.py:487
  17.6 0.0 copy-start.1
  17.6 0.9 %copy-done.1 = f32[4,96,128]{2,1,0:T(8,128)S(1)} copy-done((f32[4,96,128]{2,1,0:T(8,128)S(1)}, f32[4,96,128]{2,1,0:T(8,128)}, u32[]{:S(2)}) %copy-start.1) | copy-done | bytes 196632
  18.5 17.7 %evolve_and_gram.1 = (bf16[36,64,1024]{2,1,0:T(8,128)(2,1)S(1)}, f32[8,128]{1,0:T(8,128)S(1)}) custom-call(bf16[3,32,96,128]{3,2,1,0:T(8,128)(2,1)S(1)} %get-tuple-element.10.probes, f32[4,96,128]{2,1,0:T(8,128)S(1)} %copy-done.1, f32[100,4,128]{2,1,0:T(4,128)S(1)} %collective-permute-done.x_a, f32[100,4,128]{2,1,0:T(4,128)S(1)} %collective-permute-done.1.x_b, ...), custom_call_target="tpu_custom_call" | custom-call | tf_op jit(solution)/shard_map/evolve_and_gram/pallas_call | solution.py:364
  36.3 16.8 %all_to_all.5.grams = f32[32,8,128]{2,1,0:T(8,128)S(1)} all-to-all(f32[32,8,128]{2,1,0:T(8,128)S(1)} %broadcast_in_dim.2), channel_id=1, replica_groups=mesh['gx'=4,'gy'=8] {'gx','gy'}, dimensions={0} | all-to-all | bytes 262144 | tf_op jit(solution)/shard_map/all_to_all | solution.py:490
  53.1 8.1 %factor_and_apply.1 = (bf16[3,32,96,128]{3,2,1,0:T(8,128)(2,1)}, f32[32,32]{1,0:T(8,128)}) custom-call(f32[32,8,128]{2,1,0:T(8,128)S(1)} %all_to_all.5.grams, bf16[36,64,1024]{2,1,0:T(8,128)(2,1)S(1)} %get-tuple-element.17.halves), custom_call_target="tpu_custom_call" | custom-call | tf_op jit(solution)/shard_map/factor_and_apply/pallas_call | solution.py:440
  (6 shorter events, 0.1 us)
Async XLA Ops:
  4.0 0.7 %copy-start = (f32[4,96,128]{2,1,0:T(8,128)}, f32[4,96,128]{2,1,0:T(8,128)S(1)}, u32[]{:S(2)}) copy-start(f32[4,96,128]{2,1,0:T(8,128)S(1)} %get-tuple-element.11.coefs) | copy-start | bytes 589828
  4.7 4.5 %collective-permute-start.2 = (f32[4,96,128]{2,1,0:T(8,128)S(1)}, f32[4,96,128]{2,1,0:T(8,128)S(1)}, u32[]{:S(2)}, u32[]{:S(2)}) collective-permute-start(f32[4,96,128]{2,1,0:T(8,128)S(1)} %get-tuple-element.14.to_a), channel_id=1, source_target_pairs={{0,1},{1,0},{2,3},{3,2},{4,5},{5,4},{6,7},{7,6},{8,9},{9,8},{10,11... | collective-permute-start | bytes 589832 | tf_op jit(solution)/shard_map/ppermute | solution.py:474
  5.2 4.1 %collective-permute-start.3 = (f32[4,96,128]{2,1,0:T(8,128)S(1)}, f32[4,96,128]{2,1,0:T(8,128)S(1)}, u32[]{:S(2)}, u32[]{:S(2)}) collective-permute-start(f32[4,96,128]{2,1,0:T(8,128)S(1)} %get-tuple-element.15.to_b), channel_id=1, source_target_pairs={{1,2},{2,1},{3,4},{4,3},{5,6},{6,5},{9,10},{10,9},{11,12},{12,11},... | collective-permute-start | bytes 589832 | tf_op jit(solution)/shard_map/ppermute | solution.py:473
  5.8 9.9 %collective-permute-start = (f32[100,4,128]{2,1,0:T(4,128)}, f32[100,4,128]{2,1,0:T(4,128)S(1)}, u32[]{:S(2)}, u32[]{:S(2)}) collective-permute-start(f32[100,4,128]{2,1,0:T(4,128)} %get-tuple-element.12), channel_id=1, source_target_pairs={{0,8},{8,0},{16,24},{24,16},{1,9},{9,1},{17,25},{25,17},{2,10},{10... | collective-permute-start | bytes 614408 | tf_op jit(solution)/shard_map/ppermute | solution.py:476
  8.5 7.2 %collective-permute-start.1 = (f32[100,4,128]{2,1,0:T(4,128)}, f32[100,4,128]{2,1,0:T(4,128)S(1)}, u32[]{:S(2)}, u32[]{:S(2)}) collective-permute-start(f32[100,4,128]{2,1,0:T(4,128)} %get-tuple-element.13), channel_id=1, source_target_pairs={{8,16},{16,8},{9,17},{17,9},{10,18},{18,10},{11,19},{19,11},{12,20... | collective-permute-start | bytes 614408 | tf_op jit(solution)/shard_map/ppermute | solution.py:475
  9.3 6.4 %collective-permute-start.5 = (f32[4,4,4,128]{3,2,1,0:T(4,128)S(1)}, f32[4,4,4,128]{3,2,1,0:T(4,128)S(1)}, u32[]{:S(2)}, u32[]{:S(2)}) collective-permute-start(f32[4,4,4,128]{3,2,1,0:T(4,128)S(1)} %get-tuple-element.30), channel_id=1, source_target_pairs={{8,16},{16,8},{9,17},{17,9},{10,18},{18,10},{11,19},{19,11},{12,20... | collective-permute-start | bytes 98312 | tf_op jit(solution)/shard_map/ppermute | solution.py:486
  10.0 7.6 %collective-permute-start.4 = (f32[4,4,4,128]{3,2,1,0:T(4,128)S(1)}, f32[4,4,4,128]{3,2,1,0:T(4,128)S(1)}, u32[]{:S(2)}, u32[]{:S(2)}) collective-permute-start(f32[4,4,4,128]{3,2,1,0:T(4,128)S(1)} %get-tuple-element.31), channel_id=1, source_target_pairs={{0,8},{8,0},{16,24},{24,16},{1,9},{9,1},{17,25},{25,17},{2,10},{10... | collective-permute-start | bytes 98312 | tf_op jit(solution)/shard_map/ppermute | solution.py:487
  17.6 0.9 %copy-start.1 = (f32[4,96,128]{2,1,0:T(8,128)S(1)}, f32[4,96,128]{2,1,0:T(8,128)}, u32[]{:S(2)}) copy-start(f32[4,96,128]{2,1,0:T(8,128)} %copy-done) | copy-start | bytes 589828

commit v3 on v1

v3 whole, which is shorter than its diff:
```python
import functools
import math

import jax
import jax.numpy as jnp
from jax import lax
from jax.experimental import pallas as pl
from jax.experimental.pallas import tpu as pltpu
from jax.sharding import PartitionSpec as P

STEPS = 2
HALO = 2 * STEPS
LANES = 128
TOP = 8

time_step = 0.3
coriolis = 0.5
gravity = 1.0

MIB = 1024 * 1024
BLOCK = 8
PARTS = 2
PIVOTS = 8
WIDE = 8


def lane_ids(rows):
    return lax.broadcasted_iota(jnp.int32, (rows, LANES), 1)


def in_hbm(arrays):
    return [pltpu.with_memory_space_constraint(v, pltpu.HBM) for v in arrays]


def pack_kernel(
    probes, depth, east_flow, north_flow, land_sea,
    x_a, x_b, y_a, y_b, held, coefs, mask, sems,
):
    fields, count, rows, _ = held.shape
    even_x = lax.rem(lax.axis_index("gx"), 2) == 0
    even_y = lax.rem(lax.axis_index("gy"), 2) == 0
    small = [
        pltpu.make_async_copy(source, target, sems.at[fields + i])
        for i, (source, target) in enumerate(
            ((land_sea, mask), (depth, coefs.at[0]), (east_flow, coefs.at[1]), (north_flow, coefs.at[2]))
        )
    ]
    large = [
        pltpu.make_async_copy(probes.at[c], held.at[c], sems.at[c]) for c in range(fields)
    ]
    for copy in small + large:
        copy.start()
    for copy in small:
        copy.wait()
    lane = lane_ids(rows)
    coefs[3] = mask[...].astype(jnp.float32)

    def place(index, low, high, value):
        at = HALO * index
        turned = pltpu.roll(value, at, 1) if index else value
        low = jnp.where((lane >= at) & (lane < at + HALO), turned, low)
        back = (at - HALO) % LANES
        high = jnp.where((lane >= back) & (lane < back + HALO), turned, high)
        return low, high

    def rows_out(at, value):
        low, high = value[:HALO], value[rows - HALO :]
        x_a[at] = jnp.where(even_x, high, low)
        x_b[at] = jnp.where(even_x, low, high)

    def columns_out(at, low, high):
        y_a[at] = jnp.where(even_y, high, low)
        y_b[at] = jnp.where(even_y, low, high)

    zero = jnp.zeros((rows, LANES), jnp.float32)
    low, high = zero, zero
    for a in range(4):
        value = coefs[a]
        rows_out(fields * count + a, value)
        low, high = place(a, low, high, value)
    columns_out(fields, low, high)
    for c in range(fields):
        large[c].wait()
        low, high = zero, zero
        for p in range(count):
            value = held[c, p].astype(jnp.float32) * coefs[3]
            rows_out(c * count + p, value)
            low, high = place(p, low, high, value)
        columns_out(c, low, high)


def pack(*arguments):
    probes = arguments[0]
    fields, count, rows, cols = probes.shape
    f32 = jnp.float32
    x_shape = jax.ShapeDtypeStruct((fields * count + 4, HALO, cols), f32)
    y_shape = jax.ShapeDtypeStruct((fields + 1, rows, LANES), f32)
    return pl.pallas_call(
        pack_kernel,
        in_specs=[pl.BlockSpec(memory_space=pltpu.HBM)] * 5,
        out_shape=(
            x_shape, x_shape, y_shape, y_shape,
            jax.ShapeDtypeStruct(probes.shape, probes.dtype),
        ),
        scratch_shapes=[
            pltpu.VMEM((4, rows, cols), f32),
            pltpu.VMEM((rows, cols), jnp.int32),
            pltpu.SemaphoreType.DMA((fields + 4,)),
        ],
        compiler_params=pltpu.CompilerParams(vmem_limit_bytes=16 * MIB),
        name="pack_edges",
    )(*in_hbm(arguments))


class Grid:
    def __init__(self, rows):
        self.rows = rows
        self.own = pl.ds(TOP, rows)
        self.bottom = TOP + rows
        self.first = TOP - HALO
        self.tall = rows + 2 * HALO
        self.tiles = [self.first + 8 * t for t in range(self.tall // 8)]
        self.padded = 16 * ((self.tall + 15) // 16)
        self.window = pl.ds(self.first, self.padded)
        self.height = self.padded + TOP
        self.middle = self.tiles[1:-1]
        self.outer = [self.tiles[0], self.tiles[-1]]
        self.around = [self.tiles[0], self.tiles[1], self.tiles[-2], self.tiles[-1]]


def fold(out, at, size, values):
    deep, east, north, sea = values
    half = 0.5 * time_step
    out[0, pl.ds(at, size)] = deep
    out[1, pl.ds(at, size)] = half * sea * east
    out[2, pl.ds(at, size)] = half * sea * north
    out[3, pl.ds(at, size)] = (half * gravity) * sea


def unpack(at, size, tile_of, strip_coef, strips, fields, groups):
    back = (HALO, 0, HALO, 0)
    lane = lane_ids(size)
    part = lax.rem(lane, 16) // HALO

    def gathered(plane, slot):
        out = None
        for k in range(4):
            index = (HALO * slot + lax.rem(lane, HALO) - back[k] + LANES) & (LANES - 1)
            picked = jnp.take_along_axis(tile_of(k, plane), index, axis=1)
            out = picked if out is None else jnp.where(part == k, picked, out)
        return out

    fold(strip_coef, at, size, [gathered(fields, jnp.full_like(lane, a)) for a in range(4)])
    for c in range(fields):
        for g in range(groups):
            strips[c, g, pl.ds(at, size)] = gathered(c, 8 * g + lane // 16)


def two(value):
    top = value.astype(jnp.bfloat16)
    return top, (value - top.astype(jnp.float32)).astype(jnp.bfloat16)


def shifted(value, wrap):
    lane = lane_ids(8)
    up = value if wrap is None else jnp.where(lane == 0, wrap, value)
    down = value if wrap is None else jnp.where(lane == LANES - 1, wrap, value)
    return pltpu.roll(up, LANES - 1, 1) - pltpu.roll(down, 1, 1)


def ends():
    lane = lane_ids(8)
    return (lane == 0) | (lane == LANES - 1)


def velocities(tiles, source, factors, differences, flux, write):
    for at in tiles:
        here, above, below = pl.ds(at, 8), pl.ds(at - 1, 8), pl.ds(at + 1, 8)
        deep, east, north, slope = [factors[a, here] for a in range(4)]
        h, e, n = [source(c)[here] for c in range(3)]
        xh, xe, xn = [source(c)[below] - source(c)[above] for c in range(3)]
        yh, ye, yn = [differences(c, at, v) for c, v in enumerate((h, e, n))]
        e_new = e + (time_step * coriolis) * n - (east * xe + north * ye + slope * xh)
        n_new = n - (time_step * coriolis) * e - (east * xn + north * yn + slope * yh)
        write(at, e_new, n_new)
        flux[0, here] = deep * e_new
        flux[1, here] = deep * n_new
        flux[2, here] = h - (east * xh + north * yh)


def heights(tiles, factors, across, flux, write):
    for at in tiles:
        here, above, below = pl.ds(at, 8), pl.ds(at - 1, 8), pl.ds(at + 1, 8)
        along = flux[0, below] - flux[0, above]
        write(at, flux[2, here] - factors[3, here] * (along + across(at)))


def plain(c, at, value):
    return shifted(value, None)


def keep(edges, slot, g, at, value):
    here = lax.rem(lane_ids(8), 16) == HALO
    edges[slot, g, pl.ds(at, 8)] = jnp.where(here, pltpu.roll(value, LANES - 8, 1), value)


def keep_flux(edges, slot, g, at, value):
    here = lax.rem(lane_ids(8), 16) == HALO
    edges[slot, g, pl.ds(at, 8)] = jnp.where(
        here, -pltpu.roll(value, 1, 1), pltpu.roll(value, LANES - 9, 1)
    )


def strip_velocities(tiles, written, g, now, later, strip_coef, flux, edges, slot):
    for at in tiles:
        for c in range(3):
            keep(edges, slot + c, g, at, now[c, g, pl.ds(at, 8)])

    def write(at, e_new, n_new):
        if later is not None and at in written:
            later[1, g, pl.ds(at, 8)] = e_new
            later[2, g, pl.ds(at, 8)] = n_new

    velocities(tiles, lambda c: now.at[c, g], strip_coef, plain, flux, write)
    for at in tiles:
        keep_flux(edges, slot + 3, g, at, flux[1, pl.ds(at, 8)])


def strip_heights(tiles, g, later, strip_coef, flux):
    def write(at, h_new):
        later[0, g, pl.ds(at, 8)] = h_new

    heights(tiles, strip_coef, lambda at: shifted(flux[1, pl.ds(at, 8)], None), flux, write)


def difference_weights():
    source = lax.broadcasted_iota(jnp.int32, (2 * LANES, LANES), 0) & (LANES - 1)
    target = lax.broadcasted_iota(jnp.int32, (2 * LANES, LANES), 1)
    plus = (source == target + 1).astype(jnp.float32)
    minus = (source == target - 1).astype(jnp.float32)
    return (plus - minus).astype(jnp.bfloat16)


def flux_products(grid, flux, slope, weights):
    for k in range(WIDE):
        slope[k * grid.padded : (k + 1) * grid.padded] = jnp.dot(
            jnp.concatenate(two(flux[k, 1, grid.window]), 1),
            weights[...],
            preferred_element_type=jnp.float32,
        )


def turn_of(p):
    return lax.rem(2 * LANES - 16 * lax.rem(p, 8) - HALO, LANES)


def middle_kernel(
    probes, depth, east_flow, north_flow, land_sea, to_a, to_b, from_a, from_b,
    inner, coef, strip_coef, start, after_one,
    raw, mask, edges, weights, wraps_of, state, flux, slope, sems,
):
    fields, count, rows, _ = probes.shape
    grid = Grid(rows)
    groups = count // 8
    copies = [
        pltpu.make_async_copy(source, target, sems.at[i])
        for i, (source, target) in enumerate(
            ((land_sea, mask), (depth, raw.at[0]), (east_flow, raw.at[1]), (north_flow, raw.at[2]))
        )
    ]
    for copy in copies:
        copy.start()
    weights[...] = difference_weights()
    even_y = lax.rem(lax.axis_index("gy"), 2) == 0

    def kinds(k, *at):
        mine, theirs = (to_b, to_a) if k in (1, 2) else (from_b, from_a)
        if k in (2, 3):
            mine, theirs = theirs, mine
        return jnp.where(even_y, mine[at], theirs[at])

    for t in range(rows // 8):
        unpack(
            TOP + 8 * t, 8, lambda k, c: kinds(k, c, pl.ds(8 * t, 8)), strip_coef, start, fields, groups
        )

    def strip_body(g, carry):
        strip_velocities(
            grid.tiles, grid.middle, g, start, after_one, strip_coef, flux.at[0], edges, 0
        )
        strip_heights(grid.middle, g, after_one, strip_coef, flux.at[0])
        return carry

    lax.fori_loop(0, groups, strip_body, 0)
    for copy in copies:
        copy.wait()
    raw[3] = mask[...].astype(jnp.float32)
    fold(coef, TOP, rows, [raw[a] for a in range(4)])

    def body(i, carry):
        for k in range(WIDE):
            p = WIDE * i + k
            for c in range(fields):
                state[k, c, grid.own] = probes[c, p].astype(jnp.float32) * raw[3]
            for slot in range(4):
                for at in grid.tiles:
                    here = pl.ds(at, 8)
                    wraps_of[k, slot, here] = pltpu.roll(edges[slot, p // 8, here], turn_of(p), 1)
        for k in range(WIDE):
            p = WIDE * i + k

            def write_velocity(at, e_new, n_new):
                if at in grid.middle:
                    inner[p, 1, pl.ds(at - grid.middle[0], 8)] = e_new
                    inner[p, 2, pl.ds(at - grid.middle[0], 8)] = n_new

            velocities(
                grid.tiles, lambda c: state.at[k, c], coef,
                lambda c, at, value: shifted(value, wraps_of[k, c, pl.ds(at, 8)]),
                flux.at[k], write_velocity,
            )
        flux_products(grid, flux, slope, weights)
        for k in range(WIDE):
            p = WIDE * i + k

            def write_height(at, h_new):
                inner[p, 0, pl.ds(at - grid.middle[0], 8)] = h_new

            def across(at):
                wrap = wraps_of[k, 3, pl.ds(at, 8)]
                known = slope[pl.ds(k * grid.padded + at - grid.first, 8)]
                return known + jnp.where(ends(), wrap, 0.0)

            heights(grid.middle, coef, across, flux.at[k], write_height)
        return carry

    lax.fori_loop(0, count // WIDE, body, 0)


def middle(probes, arguments, *edges):
    fields, count, rows, cols = probes.shape
    grid = Grid(rows)
    f32, groups, height = jnp.float32, count // 8, grid.height
    full = jax.ShapeDtypeStruct((fields, groups, height, LANES), f32)
    factors = jax.ShapeDtypeStruct((4, height, LANES), f32)
    vmem, hbm = pl.BlockSpec(memory_space=pltpu.VMEM), pl.BlockSpec(memory_space=pltpu.HBM)
    return pl.pallas_call(
        middle_kernel,
        in_specs=[vmem] + [hbm] * 4 + [vmem] * 4,
        out_shape=(
            jax.ShapeDtypeStruct((count, fields, 8 * len(grid.middle), LANES), f32),
            factors, factors, full, full,
        ),
        scratch_shapes=[
            pltpu.VMEM((4, rows, cols), f32),
            pltpu.VMEM((rows, cols), jnp.int32),
            pltpu.VMEM((4, groups, height, LANES), f32),
            pltpu.VMEM((2 * LANES, LANES), jnp.bfloat16),
            pltpu.VMEM((WIDE, 4, height, LANES), f32),
            pltpu.VMEM((WIDE, fields, height, LANES), f32),
            pltpu.VMEM((WIDE, 3, height, LANES), f32),
            pltpu.VMEM((WIDE * grid.padded, LANES), f32),
            pltpu.SemaphoreType.DMA((4,)),
        ],
        compiler_params=pltpu.CompilerParams(vmem_limit_bytes=24 * MIB),
        cost_estimate=pl.CostEstimate(flops=10**8, bytes_accessed=10**7, transcendentals=0),
        name="first_step",
    )(probes, *in_hbm(arguments), *edges)


def evolve_kernel(
    probes, inner, coef_in, strip_coef_in, start_in, after_one_in, x_a, x_b, c_a, c_b,
    halves, gram, coef, strip_coef, start, after_one, edges, weights,
    wraps_of, state, later, flux, slope, grid_state, total,
):
    fields, count, rows, _ = probes.shape
    grid = Grid(rows)
    groups = count // 8
    tall, first, bottom = grid.tall, grid.first, grid.bottom
    even_x = lax.rem(lax.axis_index("gx"), 2) == 0
    weights[...] = difference_weights()

    def x_before(i):
        return jnp.where(even_x, x_b[i], x_a[i])

    def x_after(i):
        return jnp.where(even_x, x_a[i], x_b[i])

    base = fields * count
    coef[:, grid.own] = coef_in[:, grid.own]
    fold(coef, first, HALO, [x_before(base + a) for a in range(4)])
    fold(coef, bottom, HALO, [x_after(base + a) for a in range(4)])
    strip_coef[:, grid.own] = strip_coef_in[:, grid.own]
    start[:, :, pl.ds(TOP, 16)] = start_in[:, :, pl.ds(TOP, 16)]
    start[:, :, pl.ds(bottom - 16, 16)] = start_in[:, :, pl.ds(bottom - 16, 16)]
    for at in grid.middle:
        after_one[:, :, pl.ds(at, 8)] = after_one_in[:, :, pl.ds(at, 8)]
    blank = jnp.zeros((8 - HALO, LANES), jnp.float32)

    def corner(k, c, before):
        value = jnp.where(even_x == before, c_b[k, c], c_a[k, c])
        return jnp.concatenate([blank, value] if before else [value, blank], 0)

    unpack(0, 8, lambda k, c: corner(k, c, True), strip_coef, start, fields, groups)
    unpack(bottom, 8, lambda k, c: corner(k, c, False), strip_coef, start, fields, groups)

    def strip_body(g, carry):
        mine = flux.at[0]
        strip_velocities(grid.around, grid.outer, g, start, after_one, strip_coef, mine, edges, 0)
        strip_heights(grid.outer, g, after_one, strip_coef, mine)
        strip_velocities(grid.tiles, [], g, after_one, None, strip_coef, mine, edges, 4)
        return carry

    lax.fori_loop(0, groups, strip_body, 0)
    near = 24

    def body(i, carry):
        for k in range(WIDE):
            p = WIDE * i + k
            for c in range(fields):
                for at in (0, rows - near):
                    sea = coef[3, pl.ds(TOP + at, near)] != 0.0
                    value = probes[c, p, pl.ds(at, near)].astype(jnp.float32)
                    state[k, c, pl.ds(TOP + at, near)] = jnp.where(sea, value, 0.0)
                state[k, c, pl.ds(first, HALO)] = x_before(c * count + p)
                state[k, c, pl.ds(bottom, HALO)] = x_after(c * count + p)
                later[k, c, pl.ds(grid.middle[0], 8 * len(grid.middle))] = inner[p, c]
            for slot in range(4 * STEPS):
                for at in grid.around if slot < 4 else grid.tiles:
                    here = pl.ds(at, 8)
                    wraps_of[k, slot, here] = pltpu.roll(edges[slot, p // 8, here], turn_of(p), 1)

        for k in range(WIDE):

            def write_velocity(at, e_new, n_new):
                if at in grid.outer:
                    later[k, 1, pl.ds(at, 8)] = e_new
                    later[k, 2, pl.ds(at, 8)] = n_new

            def write_height(at, h_new):
                later[k, 0, pl.ds(at, 8)] = h_new

            def across(at):
                value, lane = flux[k, 1, pl.ds(at, 8)], lane_ids(8)
                up = jnp.where(lane == LANES - 1, 0.0, pltpu.roll(value, LANES - 1, 1))
                down = jnp.where(lane == 0, 0.0, pltpu.roll(value, 1, 1))
                return up - down + jnp.where(ends(), wraps_of[k, 3, pl.ds(at, 8)], 0.0)

            velocities(
                grid.around, lambda c: state.at[k, c], coef,
                lambda c, at, value: shifted(value, wraps_of[k, c, pl.ds(at, 8)]),
                flux.at[k], write_velocity,
            )
            heights(grid.outer, coef, across, flux.at[k], write_height)

        for k in range(WIDE):

            def row(c):
                return pl.multiple_of((c * count + WIDE * i + k) * tall, 8)

            def write_velocity(at, e_new, n_new):
                grid_state[pl.ds(row(1) + (at - first), 8)] = e_new
                grid_state[pl.ds(row(2) + (at - first), 8)] = n_new

            velocities(
                grid.tiles, lambda c: later.at[k, c], coef,
                lambda c, at, value: shifted(value, wraps_of[k, 4 + c, pl.ds(at, 8)]),
                flux.at[k], write_velocity,
            )
        flux_products(grid, flux, slope, weights)
        for k in range(WIDE):

            def row(c):
                return pl.multiple_of((c * count + WIDE * i + k) * tall, 8)

            def write_height(at, h_new):
                grid_state[pl.ds(row(0) + (at - first), 8)] = h_new

            def across(at):
                wrap = wraps_of[k, 7, pl.ds(at, 8)]
                return slope[pl.ds(k * grid.padded + at - first, 8)] + jnp.where(ends(), wrap, 0.0)

            heights(grid.tiles, coef, across, flux.at[k], write_height)
        return carry

    lax.fori_loop(0, count // WIDE, body, 0)

    total[...] = jnp.zeros_like(total)

    def gram_body(i, acc):
        c, block = i // (rows // BLOCK), lax.rem(i, rows // BLOCK)
        at = c * count * tall + block * BLOCK + HALO
        values = jnp.concatenate(
            [grid_state[pl.ds(at + x, count, stride=tall)] for x in range(BLOCK)], 1
        )
        top = values.astype(jnp.bfloat16)
        low = (values - top.astype(jnp.float32)).astype(jnp.bfloat16)
        both = jnp.concatenate([top, low], 0)
        halves[i] = both
        return acc + lax.dot_general(
            both, both, (((1,), (1,)), ((), ())), preferred_element_type=jnp.float32
        )

    acc = jnp.zeros((2 * count, 2 * count), jnp.float32)
    acc = lax.fori_loop(0, fields * rows // BLOCK, gram_body, acc, unroll=True)
    total[:, : 2 * count] = acc
    value = total[...]
    summed = value[:count] + value[count:]
    summed = summed + pltpu.roll(summed, LANES - count, 1)
    lane = lane_ids(count)
    summed = jnp.where(lane < count, summed, 0.0)
    out = summed[:8]
    for b in range(1, count // 8):
        out = out + pltpu.roll(summed[8 * b : 8 * b + 8], count * b, 1)
    gram[...] = out


def evolve(probes, known, *received):
    fields, count, rows, cols = probes.shape
    grid = Grid(rows)
    f32, groups, height = jnp.float32, count // 8, grid.height
    return pl.pallas_call(
        evolve_kernel,
        out_shape=(
            jax.ShapeDtypeStruct((fields * rows // BLOCK, 2 * count, BLOCK * cols), jnp.bfloat16),
            jax.ShapeDtypeStruct((8, LANES), f32),
        ),
        scratch_shapes=[
            pltpu.VMEM((4, height, LANES), f32),
            pltpu.VMEM((4, height, LANES), f32),
            pltpu.VMEM((fields, groups, height, LANES), f32),
            pltpu.VMEM((fields, groups, height, LANES), f32),
            pltpu.VMEM((4 * STEPS, groups, height, LANES), f32),
            pltpu.VMEM((2 * LANES, LANES), jnp.bfloat16),
            pltpu.VMEM((WIDE, 4 * STEPS, height, LANES), f32),
            pltpu.VMEM((WIDE, fields, height, LANES), f32),
            pltpu.VMEM((WIDE, fields, height, LANES), f32),
            pltpu.VMEM((WIDE, 3, height, LANES), f32),
            pltpu.VMEM((WIDE * grid.padded, LANES), f32),
            pltpu.VMEM((fields * count * grid.tall, LANES), f32),
            pltpu.VMEM((2 * count, LANES), f32),
        ],
        compiler_params=pltpu.CompilerParams(vmem_limit_bytes=30 * MIB),
        cost_estimate=pl.CostEstimate(flops=10**8, bytes_accessed=10**7, transcendentals=0),
        name="evolve_and_gram",
    )(probes, *known, *received)


def finish_kernel(scale, grams, halves, basis, triangle, grid_out, staged, sems):
    fields, count, rows, cols = staged.shape
    stride = grid_out.shape[0] // count
    summed = jnp.sum(grams[...], 0)
    lane = lane_ids(count)
    row_id = lax.broadcasted_iota(jnp.int32, (count, LANES), 0)
    gram = jnp.concatenate(
        [summed if b == 0 else pltpu.roll(summed, LANES - count * b, 1) for b in range(count // 8)],
        0,
    )
    work = jnp.where(lane < count, gram, jnp.where(lane == row_id + count, 1.0, 0.0))
    part = [work[8 * i : 8 * i + 8] for i in range(count // 8)]
    row8 = lax.broadcasted_iota(jnp.int32, (8, LANES), 0)

    def spread(value, k):
        return jnp.broadcast_to(value[:, k : k + 1], (8, LANES))

    for k in range(0, count, PIVOTS):
        span = range(PIVOTS)
        block = part[k // 8]
        pivot_rows = [jnp.broadcast_to(block[k % 8 + i : k % 8 + i + 1], (8, LANES)) for i in span]
        inner = [[spread(pivot_rows[j], k + i) for i in span] for j in span]
        columns = {r: [spread(part[r], k + i) for i in span] for r in range(k // 8, count // 8)}
        inverses = []
        for i in span:
            inverses.append(1.0 / inner[i][i])
            for j in range(i + 1, PIVOTS):
                ratio = inner[j][i] * inverses[i]
                pivot_rows[j] = pivot_rows[j] - ratio * pivot_rows[i]
                for m in range(i + 1, PIVOTS):
                    inner[j][m] = inner[j][m] - ratio * inner[i][m]
        for r, column in columns.items():
            ratios = []
            for i in span:
                left = column[i]
                for m in range(i):
                    left = left - ratios[m] * inner[m][i]
                left = left * inverses[i]
                if r == k // 8:
                    left = jnp.where(row8 > k % 8 + i, left, 0.0)
                ratios.append(left)
            for i in span:
                part[r] = part[r] - ratios[i] * pivot_rows[i]
    work = jnp.concatenate(part, 0)
    pivots = jnp.sum(jnp.where(lane == row_id, work, 0.0), 1, keepdims=True)
    work = work / jnp.sqrt(pivots)
    triangle[...] = jnp.where(lane >= row_id, work, 0.0)[:, :count] * (1.0 / scale)
    lower = (work * scale)[:, count : 2 * count]
    top = lower.astype(jnp.bfloat16)
    low = (lower - top.astype(jnp.float32)).astype(jnp.bfloat16)
    factor = jnp.concatenate([top, top, low], 1)

    copies = []
    for c in range(fields):

        def body(i, carry):
            both = halves[c * (rows // BLOCK) + i]
            stacked = jnp.concatenate([both, both[:count]], 0)
            out = jnp.dot(factor, stacked, preferred_element_type=jnp.float32)
            for x in range(BLOCK):
                at = BLOCK * i + x
                grid_out[pl.ds(at, count, stride=stride)] = out[:, x * cols : (x + 1) * cols]
            return carry

        lax.fori_loop(0, rows // BLOCK, body, 0, unroll=True)

        for part_of in range(PARTS):
            these = pl.ds(part_of * count // PARTS, count // PARTS)

            def store(q, carry):
                q = q + part_of * count // PARTS
                at = pl.multiple_of(q * stride, 8)
                staged[c, q] = grid_out[pl.ds(at, rows)].astype(jnp.bfloat16)
                return carry

            lax.fori_loop(0, count // PARTS, store, 0, unroll=4)
            copies.append(
                pltpu.make_async_copy(
                    staged.at[c, these], basis.at[c, these], sems.at[c * PARTS + part_of]
                )
            )
            copies[-1].start()
    for copy in copies:
        copy.wait()


def finish(grams, halves, shape, scale):
    fields, count, rows, cols = shape
    return pl.pallas_call(
        functools.partial(finish_kernel, scale),
        out_shape=(
            jax.ShapeDtypeStruct(shape, jnp.bfloat16),
            jax.ShapeDtypeStruct((count, count), jnp.float32),
        ),
        out_specs=(
            pl.BlockSpec(memory_space=pltpu.HBM),
            pl.BlockSpec(memory_space=pltpu.VMEM),
        ),
        scratch_shapes=[
            pltpu.VMEM((count * (rows + 8), cols), jnp.float32),
            pltpu.VMEM(shape, jnp.bfloat16),
            pltpu.SemaphoreType.DMA((fields * PARTS,)),
        ],
        compiler_params=pltpu.CompilerParams(vmem_limit_bytes=20 * MIB),
        name="factor_and_apply",
    )(grams, halves)


def first_pairs(size):
    return [(i, i ^ 1) for i in range(size)]


def second_pairs(size):
    return [(i, ((i + 1) ^ 1) - 1) for i in range(1, size - 1)]


def per_device(probes, depth, east_flow, north_flow, land_sea):
    fields, count, rows, cols = probes.shape
    nx, ny = lax.axis_size("gx"), lax.axis_size("gy")
    even_x = lax.rem(lax.axis_index("gx"), 2) == 0
    coefs = (depth, east_flow, north_flow, land_sea)
    x_a, x_b, to_a, to_b, held = pack(probes, *coefs)
    from_b = lax.ppermute(to_b, "gy", second_pairs(ny))
    from_a = lax.ppermute(to_a, "gy", first_pairs(ny))
    got_xb = lax.ppermute(x_b, "gx", second_pairs(nx))
    got_xa = lax.ppermute(x_a, "gx", first_pairs(nx))
    even_y = lax.rem(lax.axis_index("gy"), 2) == 0
    rows_of = (
        jnp.where(even_y, from_b, from_a),
        jnp.where(even_y, to_b, to_a),
        jnp.where(even_y, to_a, to_b),
        jnp.where(even_y, from_a, from_b),
    )
    low = jnp.stack([k[:, :HALO] for k in rows_of])
    high = jnp.stack([k[:, rows - HALO :] for k in rows_of])
    c_b = lax.ppermute(jnp.where(even_x, low, high), "gx", second_pairs(nx))
    c_a = lax.ppermute(jnp.where(even_x, high, low), "gx", first_pairs(nx))
    known = middle(held, coefs, to_a, to_b, from_a, from_b)
    halves, gram = evolve(held, known, got_xa, got_xb, c_a, c_b)
    devices = nx * ny
    grams = lax.all_to_all(
        jnp.broadcast_to(gram[None], (devices,) + gram.shape), ("gx", "gy"), 0, 0
    )
    scale = math.sqrt(fields * rows * nx * cols * ny)
    return finish(grams, halves, probes.shape, scale)


def solution(mesh):
    in_specs = (
        P(None, None, "gx", "gy"),
        P("gx", "gy"),
        P("gx", "gy"),
        P("gx", "gy"),
        P("gx", "gy"),
    )
    out_specs = (P(None, None, "gx", "gy"), P())
    return jax.shard_map(
        per_device, mesh=mesh, in_specs=in_specs, out_specs=out_specs, check_vma=False
    )
```

time: 71.3 us -> 56.1 us (0.79)
  local copies, waits for them, and re-layouts: 6.48 us -> 0.03 us
  Pallas kernels: 34 us -> 28.1 us
  waiting for transfers between devices: 1.9 us -> 0.02 us
    pallas_call x1, Pallas kernels: 23.3 us -> 12.3 us  [evolve(): pl.pallas_call(evolve_kernel, out_shape=(jax.ShapeDtypeStruct((fields * r...]
    pallas_call x0 -> x1, Pallas kernels: none -> 8.1 us  [middle(): pl.pallas_call(middle_kernel, in_specs=[vmem] + [hbm] * 4 + [vmem] * 4, o...]
    unnamed x14 -> x0, local copies, waits for them, and re-layouts: 6.45 us -> none
    pallas_call x1, Pallas kernels: 8.08 us -> 4.23 us  [finish(): pl.pallas_call(functools.partial(finish_kernel, scale), out_shape=(jax.Sh...]
    ppermute x1, waiting for transfers between devices: 1.88 us -> 0.01 us  [per_device(): c_a = lax.ppermute(jnp.where(even_x, high, low), 'gx', first_pairs(nx))]
    pallas_call x1, Pallas kernels: 2.64 us -> 3.41 us  [pack(): pl.pallas_call(pack_kernel, in_specs=[pl.BlockSpec(memory_space=pltpu.HBM...]
  transfers between devices with their start and end apart: 6 -> 6, of which waited for: 1 -> 0; matrix products, arithmetic and copies ran while one was open for 0% -> 0% of each run, Pallas kernels for 0% -> 14%
where the time goes in v3:
time: 56.1 us; the launch traced here: 55.9 us
  Pallas kernels  28.1 us (50%)
  blocking collectives  16.1 us (29%)
  starting transfers between devices  10.9 us (19%)
  between operations  0.78 us (1%)
    all_to_all x1, blocking collectives, per_device(): lax.all_to_all(jnp.broadcast_to(gram[None], (devices,) + gram.shape), ('g...  16.1 us
    pallas_call x1, Pallas kernels, evolve(): pl.pallas_call(evolve_kernel, out_shape=(jax.ShapeDtypeStruct((fields * r...  12.3 us
    pallas_call x1, Pallas kernels, middle(): pl.pallas_call(middle_kernel, in_specs=[vmem] + [hbm] * 4 + [vmem] * 4, o...  8.1 us
    ppermute x1, starting transfers between devices, per_device(): c_a = lax.ppermute(jnp.where(even_x, high, low), 'gx', first_pairs(nx))  5.71 us
    pallas_call x1, Pallas kernels, finish(): pl.pallas_call(functools.partial(finish_kernel, scale), out_shape=(jax.Sh...  4.23 us
    pallas_call x1, Pallas kernels, pack(): pl.pallas_call(pack_kernel, in_specs=[pl.BlockSpec(memory_space=pltpu.HBM...  3.41 us
    ppermute x1, starting transfers between devices, per_device(): got_xa = lax.ppermute(x_a, 'gx', first_pairs(nx))  2.66 us
  transfers between devices with their start and end apart: 6, of which 0 were waited for; matrix products, arithmetic and copies ran while one was open for 0% of the time, Pallas kernels for 14%

profile of v3, /device:TPU:0, one launch (start us, length us, event | category | flops | bytes accessed | tf_op | source)
XLA Modules:
  0.0 55.9 jit_solution(3342276663222941482)
XLA Ops:
  0.6 3.4 %pack_edges.1 = (f32[100,4,128]{2,1,0:T(4,128)}, f32[100,4,128]{2,1,0:T(4,128)}, f32[4,96,128]{2,1,0:T(8,128)S(1)}, f32[4,96,128]{2,1,0:T(8,128)S(1)}, bf16[3,32,96,128]{3,2,1,0:T(8,128)(2,1)S(1)}) custom-call(bf16[3,32,96,128]{3,2,1,0:T(8,128)(2,1)} %probes.1, f32[96,128]{1,0:T(8,128)} %depth.3, f32[96,128]{1,0:T(8,128)} %east_flow.3, ...), custom_call_target="tpu_custom_call" | custom-call | tf_op jit(solution)/shard_map/pack_edges/pallas_call | solution.py:98
  4.0 0.5 collective-permute-start
  4.6 0.7 %collective-permute-start.1 = (f32[4,96,128]{2,1,0:T(8,128)S(1)}, f32[4,96,128]{2,1,0:T(8,128)S(1)}, u32[]{:S(2)}, u32[]{:S(2)}) collective-permute-start(f32[4,96,128]{2,1,0:T(8,128)S(1)} %get-tuple-element.16.to_b), channel_id=1, source_target_pairs={{1,2},{2,1},{3,4},{4,3},{5,6},{6,5},{9,10},{10,9},{11,12},{12,11},... | collective-permute-start | bytes 589832 | tf_op jit(solution)/shard_map/ppermute | solution.py:671
  5.2 2.7 %collective-permute-start.2 = (f32[100,4,128]{2,1,0:T(4,128)}, f32[100,4,128]{2,1,0:T(4,128)S(1)}, u32[]{:S(2)}, u32[]{:S(2)}) collective-permute-start(f32[100,4,128]{2,1,0:T(4,128)} %get-tuple-element.22), channel_id=1, source_target_pairs={{0,8},{8,0},{16,24},{24,16},{1,9},{9,1},{17,25},{25,17},{2,10},{10... | collective-permute-start | bytes 614408 | tf_op jit(solution)/shard_map/ppermute | solution.py:674
  7.9 0.7 %collective-permute-start.3 = (f32[100,4,128]{2,1,0:T(4,128)}, f32[100,4,128]{2,1,0:T(4,128)S(1)}, u32[]{:S(2)}, u32[]{:S(2)}) collective-permute-start(f32[100,4,128]{2,1,0:T(4,128)} %get-tuple-element.23), channel_id=1, source_target_pairs={{8,16},{16,8},{9,17},{17,9},{10,18},{18,10},{11,19},{19,11},{12,20... | collective-permute-start | bytes 614408 | tf_op jit(solution)/shard_map/ppermute | solution.py:673
  8.6 0.0 collective-permute-done.from_a
  8.6 0.0 collective-permute-done.1.from_b
  8.7 0.7 %collective-permute-start.5 = (f32[4,4,4,128]{3,2,1,0:T(4,128)S(1)}, f32[4,4,4,128]{3,2,1,0:T(4,128)S(1)}, u32[]{:S(2)}, u32[]{:S(2)}) collective-permute-start(f32[4,4,4,128]{3,2,1,0:T(4,128)S(1)} %get-tuple-element.38), channel_id=1, source_target_pairs={{8,16},{16,8},{9,17},{17,9},{10,18},{18,10},{11,19},{19,11},{12,20... | collective-permute-start | bytes 98312 | tf_op jit(solution)/shard_map/ppermute | solution.py:684
  9.4 5.7 %collective-permute-start.4 = (f32[4,4,4,128]{3,2,1,0:T(4,128)S(1)}, f32[4,4,4,128]{3,2,1,0:T(4,128)S(1)}, u32[]{:S(2)}, u32[]{:S(2)}) collective-permute-start(f32[4,4,4,128]{3,2,1,0:T(4,128)S(1)} %get-tuple-element.39), channel_id=1, source_target_pairs={{0,8},{8,0},{16,24},{24,16},{1,9},{9,1},{17,25},{25,17},{2,10},{10... | collective-permute-start | bytes 98312 | tf_op jit(solution)/shard_map/ppermute | solution.py:685
  15.1 8.1 %first_step.1 = (f32[32,3,88,128]{3,2,1,0:T(8,128)S(1)}, f32[4,120,128]{2,1,0:T(8,128)S(1)}, f32[4,120,128]{2,1,0:T(8,128)S(1)}, f32[3,4,120,128]{3,2,1,0:T(8,128)S(1)}, f32[3,4,120,128]{3,2,1,0:T(8,128)S(1)}) custom-call(bf16[3,32,96,128]{3,2,1,0:T(8,128)(2,1)S(1)} %get-tuple-element.14.probes, f32[96,128]{1,0:T(8,128)} %depth.3, f32[96,128]{1,0:T(8,128)} %east_flow.3, ...), custom_call_target="tpu_custom_call" | custom-call | flops 100000000 | bytes 10000000 | tf_op jit(solution)/shard_map/first_step/pallas_call | solution.py:347
  23.2 0.0 collective-permute-done.2.x_a
  23.2 0.0 collective-permute-done.3.x_b
  23.2 0.0 collective-permute-done.5.c_b
  23.3 0.0 collective-permute-done.4.c_a
  23.3 12.3 %evolve_and_gram.1 = (bf16[36,64,1024]{2,1,0:T(8,128)(2,1)S(1)}, f32[8,128]{1,0:T(8,128)S(1)}) custom-call(bf16[3,32,96,128]{3,2,1,0:T(8,128)(2,1)S(1)} %get-tuple-element.14.probes, f32[32,3,88,128]{3,2,1,0:T(8,128)S(1)} %get-tuple-element.17.inner, f32[4,120,128]{2,1,0:T(8,128)S(1)} %get-tuple-element.18.coef_in, ...), custom_call_target="tpu_custom_call" | custom-call | flops 100000000 | bytes 10000000 | tf_op jit(solution)/shard_map/evolve_and_gram/pallas_call | solution.py:522
  35.6 16.1 %all_to_all.5.grams = f32[32,8,128]{2,1,0:T(8,128)S(1)} all-to-all(f32[32,8,128]{2,1,0:T(8,128)S(1)} %broadcast_in_dim.2), channel_id=1, replica_groups=mesh['gx'=4,'gy'=8] {'gx','gy'}, dimensions={0} | all-to-all | bytes 262144 | tf_op jit(solution)/shard_map/all_to_all | solution.py:689
  51.7 4.2 %factor_and_apply.1 = (bf16[3,32,96,128]{3,2,1,0:T(8,128)(2,1)}, f32[32,32]{1,0:T(8,128)}) custom-call(f32[32,8,128]{2,1,0:T(8,128)S(1)} %all_to_all.5.grams, bf16[36,64,1024]{2,1,0:T(8,128)(2,1)S(1)} %get-tuple-element.25.halves), custom_call_target="tpu_custom_call" | custom-call | tf_op jit(solution)/shard_map/factor_and_apply/pallas_call | solution.py:637
  (6 shorter events, 0.1 us)
Async XLA Ops:
  4.0 4.6 %collective-permute-start = (f32[4,96,128]{2,1,0:T(8,128)S(1)}, f32[4,96,128]{2,1,0:T(8,128)S(1)}, u32[]{:S(2)}, u32[]{:S(2)}) collective-permute-start(f32[4,96,128]{2,1,0:T(8,128)S(1)} %get-tuple-element.15.to_a), channel_id=1, source_target_pairs={{0,1},{1,0},{2,3},{3,2},{4,5},{5,4},{6,7},{7,6},{8,9},{9,8},{10,11... | collective-permute-start | bytes 589832 | tf_op jit(solution)/shard_map/ppermute | solution.py:672
  4.6 4.1 %collective-permute-start.1 = (f32[4,96,128]{2,1,0:T(8,128)S(1)}, f32[4,96,128]{2,1,0:T(8,128)S(1)}, u32[]{:S(2)}, u32[]{:S(2)}) collective-permute-start(f32[4,96,128]{2,1,0:T(8,128)S(1)} %get-tuple-element.16.to_b), channel_id=1, source_target_pairs={{1,2},{2,1},{3,4},{4,3},{5,6},{6,5},{9,10},{10,9},{11,12},{12,11},... | collective-permute-start | bytes 589832 | tf_op jit(solution)/shard_map/ppermute | solution.py:671
  5.2 18.0 %collective-permute-start.2 = (f32[100,4,128]{2,1,0:T(4,128)}, f32[100,4,128]{2,1,0:T(4,128)S(1)}, u32[]{:S(2)}, u32[]{:S(2)}) collective-permute-start(f32[100,4,128]{2,1,0:T(4,128)} %get-tuple-element.22), channel_id=1, source_target_pairs={{0,8},{8,0},{16,24},{24,16},{1,9},{9,1},{17,25},{25,17},{2,10},{10... | collective-permute-start | bytes 614408 | tf_op jit(solution)/shard_map/ppermute | solution.py:674
  7.9 15.3 %collective-permute-start.3 = (f32[100,4,128]{2,1,0:T(4,128)}, f32[100,4,128]{2,1,0:T(4,128)S(1)}, u32[]{:S(2)}, u32[]{:S(2)}) collective-permute-start(f32[100,4,128]{2,1,0:T(4,128)} %get-tuple-element.23), channel_id=1, source_target_pairs={{8,16},{16,8},{9,17},{17,9},{10,18},{18,10},{11,19},{19,11},{12,20... | collective-permute-start | bytes 614408 | tf_op jit(solution)/shard_map/ppermute | solution.py:673
  8.7 14.5 %collective-permute-start.5 = (f32[4,4,4,128]{3,2,1,0:T(4,128)S(1)}, f32[4,4,4,128]{3,2,1,0:T(4,128)S(1)}, u32[]{:S(2)}, u32[]{:S(2)}) collective-permute-start(f32[4,4,4,128]{3,2,1,0:T(4,128)S(1)} %get-tuple-element.38), channel_id=1, source_target_pairs={{8,16},{16,8},{9,17},{17,9},{10,18},{18,10},{11,19},{19,11},{12,20... | collective-permute-start | bytes 98312 | tf_op jit(solution)/shard_map/ppermute | solution.py:684
  9.4 13.8 %collective-permute-start.4 = (f32[4,4,4,128]{3,2,1,0:T(4,128)S(1)}, f32[4,4,4,128]{3,2,1,0:T(4,128)S(1)}, u32[]{:S(2)}, u32[]{:S(2)}) collective-permute-start(f32[4,4,4,128]{3,2,1,0:T(4,128)S(1)} %get-tuple-element.39), channel_id=1, source_target_pairs={{0,8},{8,0},{16,24},{24,16},{1,9},{9,1},{17,25},{25,17},{2,10},{10... | collective-permute-start | bytes 98312 | tf_op jit(solution)/shard_map/ppermute | solution.py:685

commit v4 on v3

--- a/solution.py
+++ b/solution.py
@@ -182,10 +182,10 @@
         yh, ye, yn = [differences(c, at, v) for c, v in enumerate((h, e, n))]
         e_new = e + (time_step * coriolis) * n - (east * xe + north * ye + slope * xh)
         n_new = n - (time_step * coriolis) * e - (east * xn + north * yn + slope * yh)
-        write(at, e_new, n_new)
         flux[0, here] = deep * e_new
         flux[1, here] = deep * n_new
         flux[2, here] = h - (east * xh + north * yh)
+        write(at, e_new, n_new)
 
 
 def heights(tiles, factors, across, flux, write):
@@ -205,14 +205,33 @@
 
 
 def keep_flux(edges, slot, g, at, value):
+    edges[slot, g, pl.ds(at, 8)] = lacking(value)
+
+
+def lacking(value):
     here = lax.rem(lane_ids(8), 16) == HALO
-    edges[slot, g, pl.ds(at, 8)] = jnp.where(
-        here, -pltpu.roll(value, 1, 1), pltpu.roll(value, LANES - 9, 1)
-    )
-
-
-def strip_velocities(tiles, written, g, now, later, strip_coef, flux, edges, slot):
+    return jnp.where(here, -pltpu.roll(value, 1, 1), pltpu.roll(value, LANES - 9, 1))
+
+
+def beside(value):
+    here = lax.rem(lane_ids(8), 16) == HALO
+    return jnp.where(here, value, pltpu.roll(value, LANES - 8, 1))
+
+
+def keep_lacking(edges, g, at, now, strip_coef):
+    here = pl.ds(at, 8)
+    north, slope = beside(strip_coef[2, here]), beside(strip_coef[3, here])
+    h, e, n = [lacking(now[c, g, here]) for c in range(3)]
+    edges[0, g, here] = -north * h
+    edges[1, g, here] = -north * e
+    edges[2, g, here] = -(north * n + slope * h)
+
+
+def strip_velocities(tiles, written, g, now, later, strip_coef, flux, edges, slot, alone=False):
     for at in tiles:
+        if alone:
+            keep_lacking(edges, g, at, now, strip_coef)
+            continue
         for c in range(3):
             keep(edges, slot + c, g, at, now[c, g, pl.ds(at, 8)])
 
@@ -254,14 +273,12 @@
     return lax.rem(2 * LANES - 16 * lax.rem(p, 8) - HALO, LANES)
 
 
-def middle_kernel(
-    probes, depth, east_flow, north_flow, land_sea, to_a, to_b, from_a, from_b,
-    inner, coef, strip_coef, start, after_one,
-    raw, mask, edges, weights, wraps_of, state, flux, slope, sems,
+def alone_kernel(
+    probes, depth, east_flow, north_flow, land_sea, first_e, first_n, first_h, coef,
+    raw, mask, state, flux, sems,
 ):
     fields, count, rows, _ = probes.shape
     grid = Grid(rows)
-    groups = count // 8
     copies = [
         pltpu.make_async_copy(source, target, sems.at[i])
         for i, (source, target) in enumerate(
@@ -270,6 +287,94 @@
     ]
     for copy in copies:
         copy.start()
+    for copy in copies:
+        copy.wait()
+    raw[3] = mask[...].astype(jnp.float32)
+    fold(coef, TOP, rows, [raw[a] for a in range(4)])
+    lane = lane_ids(8)
+
+    def differences(c, at, value):
+        up = jnp.where(lane == LANES - 1, 0.0, pltpu.roll(value, LANES - 1, 1))
+        return up - jnp.where(lane == 0, 0.0, pltpu.roll(value, 1, 1))
+
+    def body(i, carry):
+        for k in range(WIDE):
+            p = WIDE * i + k
+            for c in range(fields):
+                state[k, c, grid.own] = probes[c, p].astype(jnp.float32) * raw[3]
+        for k in range(WIDE):
+            p = WIDE * i + k
+
+            def write(at, e_new, n_new):
+                first_e[p, pl.ds(at - grid.first, 8)] = e_new
+                first_n[p, pl.ds(at - grid.first, 8)] = n_new
+                first_h[p, pl.ds(at - grid.first, 8)] = flux[k, 2, pl.ds(at, 8)]
+
+            velocities(
+                grid.tiles, lambda c: state.at[k, c], coef, differences, flux.at[k], write
+            )
+        return carry
+
+    lax.fori_loop(0, count // WIDE, body, 0)
+
+
+def alone(probes, arguments):
+    fields, count, rows, cols = probes.shape
+    grid = Grid(rows)
+    f32, height = jnp.float32, grid.height
+    vmem, hbm = pl.BlockSpec(memory_space=pltpu.VMEM), pl.BlockSpec(memory_space=pltpu.HBM)
+    one = jax.ShapeDtypeStruct((count, grid.tall, LANES), f32)
+    return pl.pallas_call(
+        alone_kernel,
+        in_specs=[vmem] + [hbm] * 4,
+        out_shape=(one, one, one, jax.ShapeDtypeStruct((4, height, LANES), f32)),
+        scratch_shapes=[
+            pltpu.VMEM((4, rows, cols), f32),
+            pltpu.VMEM((rows, cols), jnp.int32),
+            pltpu.VMEM((WIDE, fields, height, LANES), f32),
+            pltpu.VMEM((WIDE, 3, height, LANES), f32),
+            pltpu.SemaphoreType.DMA((4,)),
+        ],
+        compiler_params=pltpu.CompilerParams(vmem_limit_bytes=20 * MIB),
+        cost_estimate=pl.CostEstimate(flops=10**8, bytes_accessed=10**7, transcendentals=0),
+        name="first_velocities",
+    )(probes, *in_hbm(arguments))
+
+
+def corner_kernel(to_a, to_b, from_a, from_b, unused, c_a, c_b):
+    planes, rows, _ = to_a.shape
+    even_x = lax.rem(lax.axis_index("gx"), 2) == 0
+    even_y = lax.rem(lax.axis_index("gy"), 2) == 0
+    for k, (yes, no) in enumerate(((from_b, from_a), (to_b, to_a), (to_a, to_b), (from_a, from_b))):
+        for c in range(planes):
+            low = jnp.where(even_y, yes[c, pl.ds(0, HALO)], no[c, pl.ds(0, HALO)])
+            end = pl.ds(rows - HALO, HALO)
+            high = jnp.where(even_y, yes[c, end], no[c, end])
+            c_a[k, c] = jnp.where(even_x, high, low)
+            c_b[k, c] = jnp.where(even_x, low, high)
+
+
+def corners(edges, before):
+    shape = jax.ShapeDtypeStruct((4, edges[0].shape[0], HALO, LANES), jnp.float32)
+    vmem, anywhere = pl.BlockSpec(memory_space=pltpu.VMEM), pl.BlockSpec(memory_space=pl.ANY)
+    return pl.pallas_call(
+        corner_kernel,
+        in_specs=[vmem] * 4 + [anywhere],
+        out_shape=(shape, shape),
+        compiler_params=pltpu.CompilerParams(vmem_limit_bytes=8 * MIB),
+        name="corner_rows",
+    )(*edges, before)
+
+
+def middle_kernel(
+    first_e, first_n, first_h, coef, to_a, to_b, from_a, from_b,
+    inner, strip_coef, start, after_one,
+    edges, weights, wraps_of, flux, slope,
+):
+    count, fields = first_e.shape[0], to_a.shape[0] - 1
+    rows = to_a.shape[1]
+    grid = Grid(rows)
+    groups = count // 8
     weights[...] = difference_weights()
     even_y = lax.rem(lax.axis_index("gy"), 2) == 0
 
@@ -286,39 +391,35 @@
 
     def strip_body(g, carry):
         strip_velocities(
-            grid.tiles, grid.middle, g, start, after_one, strip_coef, flux.at[0], edges, 0
+            grid.tiles, grid.middle, g, start, after_one, strip_coef, flux.at[0], edges, 0, True
         )
         strip_heights(grid.middle, g, after_one, strip_coef, flux.at[0])
         return carry
 
     lax.fori_loop(0, groups, strip_body, 0)
-    for copy in copies:
-        copy.wait()
-    raw[3] = mask[...].astype(jnp.float32)
-    fold(coef, TOP, rows, [raw[a] for a in range(4)])
 
     def body(i, carry):
         for k in range(WIDE):
             p = WIDE * i + k
-            for c in range(fields):
-                state[k, c, grid.own] = probes[c, p].astype(jnp.float32) * raw[3]
             for slot in range(4):
                 for at in grid.tiles:
                     here = pl.ds(at, 8)
                     wraps_of[k, slot, here] = pltpu.roll(edges[slot, p // 8, here], turn_of(p), 1)
         for k in range(WIDE):
             p = WIDE * i + k
-
-            def write_velocity(at, e_new, n_new):
+            for at in grid.tiles:
+                here, there = pl.ds(at, 8), pl.ds(at - grid.first, 8)
+                h, e, n = [
+                    first[p, there] + jnp.where(ends(), wraps_of[k, c, here], 0.0)
+                    for c, first in enumerate((first_h, first_e, first_n))
+                ]
+                deep = coef[0, here]
+                flux[k, 0, here] = deep * e
+                flux[k, 1, here] = deep * n
+                flux[k, 2, here] = h
                 if at in grid.middle:
-                    inner[p, 1, pl.ds(at - grid.middle[0], 8)] = e_new
-                    inner[p, 2, pl.ds(at - grid.middle[0], 8)] = n_new
-
-            velocities(
-                grid.tiles, lambda c: state.at[k, c], coef,
-                lambda c, at, value: shifted(value, wraps_of[k, c, pl.ds(at, 8)]),
-                flux.at[k], write_velocity,
-            )
+                    inner[p, 1, pl.ds(at - grid.middle[0], 8)] = e
+                    inner[p, 2, pl.ds(at - grid.middle[0], 8)] = n
         flux_products(grid, flux, slope, weights)
         for k in range(WIDE):
             p = WIDE * i + k
@@ -337,35 +438,31 @@
     lax.fori_loop(0, count // WIDE, body, 0)
 
 
-def middle(probes, arguments, *edges):
-    fields, count, rows, cols = probes.shape
+def middle(firsts, coef, *edges):
+    fields, rows = edges[0].shape[0] - 1, edges[0].shape[1]
+    count = firsts[0].shape[0]
     grid = Grid(rows)
     f32, groups, height = jnp.float32, count // 8, grid.height
     full = jax.ShapeDtypeStruct((fields, groups, height, LANES), f32)
-    factors = jax.ShapeDtypeStruct((4, height, LANES), f32)
-    vmem, hbm = pl.BlockSpec(memory_space=pltpu.VMEM), pl.BlockSpec(memory_space=pltpu.HBM)
     return pl.pallas_call(
         middle_kernel,
-        in_specs=[vmem] + [hbm] * 4 + [vmem] * 4,
         out_shape=(
             jax.ShapeDtypeStruct((count, fields, 8 * len(grid.middle), LANES), f32),
-            factors, factors, full, full,
+            jax.ShapeDtypeStruct((4, height, LANES), f32),
+            full,
+            full,
         ),
         scratch_shapes=[
-            pltpu.VMEM((4, rows, cols), f32),
-            pltpu.VMEM((rows, cols), jnp.int32),
             pltpu.VMEM((4, groups, height, LANES), f32),
             pltpu.VMEM((2 * LANES, LANES), jnp.bfloat16),
             pltpu.VMEM((WIDE, 4, height, LANES), f32),
-            pltpu.VMEM((WIDE, fields, height, LANES), f32),
             pltpu.VMEM((WIDE, 3, height, LANES), f32),
             pltpu.VMEM((WIDE * grid.padded, LANES), f32),
-            pltpu.SemaphoreType.DMA((4,)),
         ],
         compiler_params=pltpu.CompilerParams(vmem_limit_bytes=24 * MIB),
         cost_estimate=pl.CostEstimate(flops=10**8, bytes_accessed=10**7, transcendentals=0),
         name="first_step",
-    )(probes, *in_hbm(arguments), *edges)
+    )(*firsts, coef, *edges)
 
 
 def evolve_kernel(
@@ -665,26 +762,18 @@
 def per_device(probes, depth, east_flow, north_flow, land_sea):
     fields, count, rows, cols = probes.shape
     nx, ny = lax.axis_size("gx"), lax.axis_size("gy")
-    even_x = lax.rem(lax.axis_index("gx"), 2) == 0
     coefs = (depth, east_flow, north_flow, land_sea)
     x_a, x_b, to_a, to_b, held = pack(probes, *coefs)
     from_b = lax.ppermute(to_b, "gy", second_pairs(ny))
     from_a = lax.ppermute(to_a, "gy", first_pairs(ny))
     got_xb = lax.ppermute(x_b, "gx", second_pairs(nx))
     got_xa = lax.ppermute(x_a, "gx", first_pairs(nx))
-    even_y = lax.rem(lax.axis_index("gy"), 2) == 0
-    rows_of = (
-        jnp.where(even_y, from_b, from_a),
-        jnp.where(even_y, to_b, to_a),
-        jnp.where(even_y, to_a, to_b),
-        jnp.where(even_y, from_a, from_b),
-    )
-    low = jnp.stack([k[:, :HALO] for k in rows_of])
-    high = jnp.stack([k[:, rows - HALO :] for k in rows_of])
-    c_b = lax.ppermute(jnp.where(even_x, low, high), "gx", second_pairs(nx))
-    c_a = lax.ppermute(jnp.where(even_x, high, low), "gx", first_pairs(nx))
-    known = middle(held, coefs, to_a, to_b, from_a, from_b)
-    halves, gram = evolve(held, known, got_xa, got_xb, c_a, c_b)
+    *firsts, coef = alone(held, coefs)
+    low_high = corners((to_a, to_b, from_a, from_b), firsts[0])
+    c_b = lax.ppermute(low_high[1], "gx", second_pairs(nx))
+    c_a = lax.ppermute(low_high[0], "gx", first_pairs(nx))
+    inner, *strip_arrays = middle(firsts, coef, to_a, to_b, from_a, from_b)
+    halves, gram = evolve(held, (inner, coef, *strip_arrays), got_xa, got_xb, c_a, c_b)
     devices = nx * ny
     grams = lax.all_to_all(
         jnp.broadcast_to(gram[None], (devices,) + gram.shape), ("gx", "gy"), 0, 0

time: 56.1 us -> 54.5 us (0.971)
  starting transfers between devices: 10.9 us -> 9.61 us
  blocking collectives: 16.1 us -> 14.9 us
  Pallas kernels: 28.1 us -> 29 us
    pallas_call x1 -> x3, Pallas kernels: 8.1 us -> 9.64 us  [the longest x1 5.62 us: middle(): pl.pallas_call(middle_kernel, out_shape=(jax.ShapeDtypeStruct((count, fie...]
    ppermute x2, starting transfers between devices: 6.37 us -> 5.1 us  [the longest x1 4.45 us: per_device(): c_a = lax.ppermute(low_high[0], 'gx', first_pairs(nx))]
    all_to_all x1, blocking collectives: 16.1 us -> 14.9 us  [per_device(): lax.all_to_all(jnp.broadcast_to(gram[None], (devices,) + gram.shape), ('g...]
    pallas_call x1, Pallas kernels: 3.41 us -> 2.78 us  [pack(): pl.pallas_call(pack_kernel, in_specs=[pl.BlockSpec(memory_space=pltpu.HBM...]
  transfers between devices with their start and end apart: 6 -> 6, of which waited for: 0 -> 0; matrix products, arithmetic and copies ran while one was open for 0% -> 0% of each run, Pallas kernels for 14% -> 18%
where the time goes in v4:
time: 54.5 us; the launch traced here: 54.2 us
  Pallas kernels  29 us (53%)
  blocking collectives  14.9 us (27%)
  starting transfers between devices  9.61 us (18%)
  between operations  0.74 us (1%)
    all_to_all x1, blocking collectives, per_device(): lax.all_to_all(jnp.broadcast_to(gram[None], (devices,) + gram.shape), ('g...  14.9 us
    pallas_call x1, Pallas kernels, evolve(): pl.pallas_call(evolve_kernel, out_shape=(jax.ShapeDtypeStruct((fields * r...  12.3 us
    pallas_call x1, Pallas kernels, middle(): pl.pallas_call(middle_kernel, out_shape=(jax.ShapeDtypeStruct((count, fie...  5.62 us
    ppermute x1, starting transfers between devices, per_device(): c_a = lax.ppermute(low_high[0], 'gx', first_pairs(nx))  4.45 us
    pallas_call x1, Pallas kernels, finish(): pl.pallas_call(functools.partial(finish_kernel, scale), out_shape=(jax.Sh...  4.23 us
    pallas_call x1, Pallas kernels, alone(): pl.pallas_call(alone_kernel, in_specs=[vmem] + [hbm] * 4, out_shape=(one,...  3.99 us
    pallas_call x1, Pallas kernels, pack(): pl.pallas_call(pack_kernel, in_specs=[pl.BlockSpec(memory_space=pltpu.HBM...  2.78 us
    ppermute x1, starting transfers between devices, per_device(): got_xa = lax.ppermute(x_a, 'gx', first_pairs(nx))  2.66 us
  transfers between devices with their start and end apart: 6, of which 0 were waited for; matrix products, arithmetic and copies ran while one was open for 0% of the time, Pallas kernels for 18%

profile of v4, /device:TPU:0, one launch (start us, length us, event | category | flops | bytes accessed | tf_op | source)
XLA Modules:
  0.0 54.2 jit_solution(1477319469611484873)
XLA Ops:
  0.6 2.8 %pack_edges.1 = (f32[100,4,128]{2,1,0:T(4,128)S(1)}, f32[100,4,128]{2,1,0:T(4,128)S(1)}, f32[4,96,128]{2,1,0:T(8,128)S(1)}, f32[4,96,128]{2,1,0:T(8,128)S(1)}, bf16[3,32,96,128]{3,2,1,0:T(8,128)(2,1)S(1)}) custom-call(bf16[3,32,96,128]{3,2,1,0:T(8,128)(2,1)} %probes.1, f32[96,128]{1,0:T(8,128)} %depth.3, f32[96,128]{1,0:T(8,128)} %east_flow.3, ...), custom_call_target="tpu_custom_call" | custom-call | tf_op jit(solution)/shard_map/pack_edges/pallas_call | solution.py:98
  3.4 0.5 collective-permute-start
  3.9 0.7 %collective-permute-start.1 = (f32[4,96,128]{2,1,0:T(8,128)S(1)}, f32[4,96,128]{2,1,0:T(8,128)S(1)}, u32[]{:S(2)}, u32[]{:S(2)}) collective-permute-start(f32[4,96,128]{2,1,0:T(8,128)S(1)} %get-tuple-element.25.to_b), channel_id=1, source_target_pairs={{1,2},{2,1},{3,4},{4,3},{5,6},{6,5},{9,10},{10,9},{11,12},{12,11},... | collective-permute-start | bytes 589832 | tf_op jit(solution)/shard_map/ppermute | solution.py:767
  4.6 2.7 %collective-permute-start.2 = (f32[100,4,128]{2,1,0:T(4,128)S(1)}, f32[100,4,128]{2,1,0:T(4,128)S(1)}, u32[]{:S(2)}, u32[]{:S(2)}) collective-permute-start(f32[100,4,128]{2,1,0:T(4,128)S(1)} %get-tuple-element.30), channel_id=1, source_target_pairs={{0,8},{8,0},{16,24},{24,16},{1,9},{9,1},{17,25},{25,17},{2,10},{10... | collective-permute-start | bytes 614408 | tf_op jit(solution)/shard_map/ppermute | solution.py:770
  7.3 0.7 %collective-permute-start.3 = (f32[100,4,128]{2,1,0:T(4,128)S(1)}, f32[100,4,128]{2,1,0:T(4,128)S(1)}, u32[]{:S(2)}, u32[]{:S(2)}) collective-permute-start(f32[100,4,128]{2,1,0:T(4,128)S(1)} %get-tuple-element.31), channel_id=1, source_target_pairs={{8,16},{16,8},{9,17},{17,9},{10,18},{18,10},{11,19},{19,11},{12,20... | collective-permute-start | bytes 614408 | tf_op jit(solution)/shard_map/ppermute | solution.py:769
  7.9 4.0 %first_velocities.1 = (f32[32,104,128]{2,1,0:T(8,128)S(1)}, f32[32,104,128]{2,1,0:T(8,128)S(1)}, f32[32,104,128]{2,1,0:T(8,128)S(1)}, f32[4,120,128]{2,1,0:T(8,128)S(1)}) custom-call(bf16[3,32,96,128]{3,2,1,0:T(8,128)(2,1)S(1)} %get-tuple-element.19.probes, f32[96,128]{1,0:T(8,128)} %depth.3, f32[96,128]{1,0:T(8,128)} %east_flow.3, f32[96,128]{1,0:T(8,128)} %north_flow.3, ...), custom_call_target="tpu_custom_call" | custom-call | flops 100000000 | bytes 10000000 | tf_op jit(solution)/shard_map/first_velocities/pallas_call | solution.py:327
  11.9 0.0 collective-permute-done.from_a
  11.9 0.0 collective-permute-done.1.from_b
  12.0 4.5 %collective-permute-start.4 = (f32[4,4,4,128]{3,2,1,0:T(4,128)S(1)}, f32[4,4,4,128]{3,2,1,0:T(4,128)S(1)}, u32[]{:S(2)}, u32[]{:S(2)}) collective-permute-start(f32[4,4,4,128]{3,2,1,0:T(4,128)S(1)} %get-tuple-element.32), channel_id=1, source_target_pairs={{0,8},{8,0},{16,24},{24,16},{1,9},{9,1},{17,25},{25,17},{2,10},{10... | collective-permute-start | bytes 98312 | tf_op jit(solution)/shard_map/ppermute | solution.py:774
  16.4 0.7 %collective-permute-start.5 = (f32[4,4,4,128]{3,2,1,0:T(4,128)S(1)}, f32[4,4,4,128]{3,2,1,0:T(4,128)S(1)}, u32[]{:S(2)}, u32[]{:S(2)}) collective-permute-start(f32[4,4,4,128]{3,2,1,0:T(4,128)S(1)} %get-tuple-element.33), channel_id=1, source_target_pairs={{8,16},{16,8},{9,17},{17,9},{10,18},{18,10},{11,19},{19,11},{12,20... | collective-permute-start | bytes 98312 | tf_op jit(solution)/shard_map/ppermute | solution.py:773
  17.1 5.6 %first_step.1 = (f32[32,3,88,128]{3,2,1,0:T(8,128)S(1)}, f32[4,120,128]{2,1,0:T(8,128)S(1)}, f32[3,4,120,128]{3,2,1,0:T(8,128)S(1)}, f32[3,4,120,128]{3,2,1,0:T(8,128)S(1)}) custom-call(f32[32,104,128]{2,1,0:T(8,128)S(1)} %get-tuple-element.20.first_e.unused, f32[32,104,128]{2,1,0:T(8,128)S(1)} %get-tuple-element.21.first_n, ...), custom_call_target="tpu_custom_call" | custom-call | flops 100000000 | bytes 10000000 | tf_op jit(solution)/shard_map/first_step/pallas_call | solution.py:447
  22.7 0.0 collective-permute-done.2.x_a
  22.7 0.0 collective-permute-done.3.x_b
  22.7 0.0 collective-permute-done.4.c_a
  22.8 0.0 collective-permute-done.5.c_b
  22.8 12.3 %evolve_and_gram.1 = (bf16[36,64,1024]{2,1,0:T(8,128)(2,1)S(1)}, f32[8,128]{1,0:T(8,128)S(1)}) custom-call(bf16[3,32,96,128]{3,2,1,0:T(8,128)(2,1)S(1)} %get-tuple-element.19.probes, f32[32,3,88,128]{3,2,1,0:T(8,128)S(1)} %get-tuple-element.26.inner, f32[4,120,128]{2,1,0:T(8,128)S(1)} %get-tuple-element.23.coef.coef_in, ...), custom_call_target="tpu_custom_call" | custom-call | flops 100000000 | bytes 10000000 | tf_op jit(solution)/shard_map/evolve_and_gram/pallas_call | solution.py:619
  35.1 14.9 %all_to_all.5.grams = f32[32,8,128]{2,1,0:T(8,128)S(1)} all-to-all(f32[32,8,128]{2,1,0:T(8,128)S(1)} %broadcast_in_dim.2), channel_id=1, replica_groups=mesh['gx'=4,'gy'=8] {'gx','gy'}, dimensions={0} | all-to-all | bytes 262144 | tf_op jit(solution)/shard_map/all_to_all | solution.py:778
  50.0 4.2 %factor_and_apply.1 = (bf16[3,32,96,128]{3,2,1,0:T(8,128)(2,1)}, f32[32,32]{1,0:T(8,128)}) custom-call(f32[32,8,128]{2,1,0:T(8,128)S(1)} %all_to_all.5.grams, bf16[36,64,1024]{2,1,0:T(8,128)(2,1)S(1)} %get-tuple-element.35.halves), custom_call_target="tpu_custom_call" | custom-call | tf_op jit(solution)/shard_map/factor_and_apply/pallas_call | solution.py:734
  (2 shorter events, 0.0 us)
Async XLA Ops:
  3.4 8.5 %collective-permute-start = (f32[4,96,128]{2,1,0:T(8,128)S(1)}, f32[4,96,128]{2,1,0:T(8,128)S(1)}, u32[]{:S(2)}, u32[]{:S(2)}) collective-permute-start(f32[4,96,128]{2,1,0:T(8,128)S(1)} %get-tuple-element.24.to_a), channel_id=1, source_target_pairs={{0,1},{1,0},{2,3},{3,2},{4,5},{5,4},{6,7},{7,6},{8,9},{9,8},{10,11... | collective-permute-start | bytes 589832 | tf_op jit(solution)/shard_map/ppermute | solution.py:768
  3.9 8.0 %collective-permute-start.1 = (f32[4,96,128]{2,1,0:T(8,128)S(1)}, f32[4,96,128]{2,1,0:T(8,128)S(1)}, u32[]{:S(2)}, u32[]{:S(2)}) collective-permute-start(f32[4,96,128]{2,1,0:T(8,128)S(1)} %get-tuple-element.25.to_b), channel_id=1, source_target_pairs={{1,2},{2,1},{3,4},{4,3},{5,6},{6,5},{9,10},{10,9},{11,12},{12,11},... | collective-permute-start | bytes 589832 | tf_op jit(solution)/shard_map/ppermute | solution.py:767
  4.6 18.1 %collective-permute-start.2 = (f32[100,4,128]{2,1,0:T(4,128)S(1)}, f32[100,4,128]{2,1,0:T(4,128)S(1)}, u32[]{:S(2)}, u32[]{:S(2)}) collective-permute-start(f32[100,4,128]{2,1,0:T(4,128)S(1)} %get-tuple-element.30), channel_id=1, source_target_pairs={{0,8},{8,0},{16,24},{24,16},{1,9},{9,1},{17,25},{25,17},{2,10},{10... | collective-permute-start | bytes 614408 | tf_op jit(solution)/shard_map/ppermute | solution.py:770
  7.3 15.5 %collective-permute-start.3 = (f32[100,4,128]{2,1,0:T(4,128)S(1)}, f32[100,4,128]{2,1,0:T(4,128)S(1)}, u32[]{:S(2)}, u32[]{:S(2)}) collective-permute-start(f32[100,4,128]{2,1,0:T(4,128)S(1)} %get-tuple-element.31), channel_id=1, source_target_pairs={{8,16},{16,8},{9,17},{17,9},{10,18},{18,10},{11,19},{19,11},{12,20... | collective-permute-start | bytes 614408 | tf_op jit(solution)/shard_map/ppermute | solution.py:769
  12.0 10.8 %collective-permute-start.4 = (f32[4,4,4,128]{3,2,1,0:T(4,128)S(1)}, f32[4,4,4,128]{3,2,1,0:T(4,128)S(1)}, u32[]{:S(2)}, u32[]{:S(2)}) collective-permute-start(f32[4,4,4,128]{3,2,1,0:T(4,128)S(1)} %get-tuple-element.32), channel_id=1, source_target_pairs={{0,8},{8,0},{16,24},{24,16},{1,9},{9,1},{17,25},{25,17},{2,10},{10... | collective-permute-start | bytes 98312 | tf_op jit(solution)/shard_map/ppermute | solution.py:774
  16.4 6.3 %collective-permute-start.5 = (f32[4,4,4,128]{3,2,1,0:T(4,128)S(1)}, f32[4,4,4,128]{3,2,1,0:T(4,128)S(1)}, u32[]{:S(2)}, u32[]{:S(2)}) collective-permute-start(f32[4,4,4,128]{3,2,1,0:T(4,128)S(1)} %get-tuple-element.33), channel_id=1, source_target_pairs={{8,16},{16,8},{9,17},{17,9},{10,18},{18,10},{11,19},{19,11},{12,20... | collective-permute-start | bytes 98312 | tf_op jit(solution)/shard_map/ppermute | solution.py:773

commit v5 on v4

--- a/solution.py
+++ b/solution.py
@@ -20,6 +20,8 @@
 MIB = 1024 * 1024
 BLOCK = 8
 PARTS = 2
+FIRST = (0, 1)
+SECOND = (0, 1, 2)
 PIVOTS = 8
 WIDE = 8
 
@@ -125,7 +127,7 @@
         self.height = self.padded + TOP
         self.middle = self.tiles[1:-1]
         self.outer = [self.tiles[0], self.tiles[-1]]
-        self.around = [self.tiles[0], self.tiles[1], self.tiles[-2], self.tiles[-1]]
+        self.beside_outer = [self.tiles[1], self.tiles[-2]]
 
 
 def fold(out, at, size, values):
@@ -227,13 +229,14 @@
     edges[2, g, here] = -(north * n + slope * h)
 
 
-def strip_velocities(tiles, written, g, now, later, strip_coef, flux, edges, slot, alone=False):
+def strip_velocities(tiles, written, g, now, later, strip_coef, flux, edges, slot, alone=False, lack=()):
     for at in tiles:
         if alone:
             keep_lacking(edges, g, at, now, strip_coef)
             continue
         for c in range(3):
-            keep(edges, slot + c, g, at, now[c, g, pl.ds(at, 8)])
+            save = keep_flux if c in lack else keep
+            save(edges, slot + c, g, at, now[c, g, pl.ds(at, 8)])
 
     def write(at, e_new, n_new):
         if later is not None and at in written:
@@ -258,6 +261,16 @@
     plus = (source == target + 1).astype(jnp.float32)
     minus = (source == target - 1).astype(jnp.float32)
     return (plus - minus).astype(jnp.bfloat16)
+
+
+def field_products(grid, source, slope, weights, chosen):
+    for j, c in enumerate(chosen):
+        for k in range(WIDE):
+            slope[j, k * grid.padded : (k + 1) * grid.padded] = jnp.dot(
+                jnp.concatenate(two(source[k, c, grid.window]), 1),
+                weights[...],
+                preferred_element_type=jnp.float32,
+            )
 
 
 def flux_products(grid, flux, slope, weights):
@@ -275,7 +288,7 @@
 
 def alone_kernel(
     probes, depth, east_flow, north_flow, land_sea, first_e, first_n, first_h, coef,
-    raw, mask, state, flux, sems,
+    raw, mask, state, flux, slope, weights, sems,
 ):
     fields, count, rows, _ = probes.shape
     grid = Grid(rows)
@@ -292,8 +305,11 @@
     raw[3] = mask[...].astype(jnp.float32)
     fold(coef, TOP, rows, [raw[a] for a in range(4)])
     lane = lane_ids(8)
-
-    def differences(c, at, value):
+    weights[...] = difference_weights()[:LANES]
+
+    def differences(k, c, at, value):
+        if c in FIRST:
+            return slope[FIRST.index(c), pl.ds(k * grid.padded + at - grid.first, 8)]
         up = jnp.where(lane == LANES - 1, 0.0, pltpu.roll(value, LANES - 1, 1))
         return up - jnp.where(lane == 0, 0.0, pltpu.roll(value, 1, 1))
 
@@ -302,6 +318,13 @@
             p = WIDE * i + k
             for c in range(fields):
                 state[k, c, grid.own] = probes[c, p].astype(jnp.float32) * raw[3]
+        for j, c in enumerate(FIRST):
+            for k in range(WIDE):
+                slope[j, k * grid.padded : (k + 1) * grid.padded] = jnp.dot(
+                    state[k, c, grid.window].astype(jnp.bfloat16),
+                    weights[...],
+                    preferred_element_type=jnp.float32,
+                )
         for k in range(WIDE):
             p = WIDE * i + k
 
@@ -311,7 +334,8 @@
                 first_h[p, pl.ds(at - grid.first, 8)] = flux[k, 2, pl.ds(at, 8)]
 
             velocities(
-                grid.tiles, lambda c: state.at[k, c], coef, differences, flux.at[k], write
+                grid.tiles, lambda c: state.at[k, c], coef,
+                functools.partial(differences, k), flux.at[k], write,
             )
         return carry
 
@@ -333,6 +357,8 @@
             pltpu.VMEM((rows, cols), jnp.int32),
             pltpu.VMEM((WIDE, fields, height, LANES), f32),
             pltpu.VMEM((WIDE, 3, height, LANES), f32),
+            pltpu.VMEM((max(len(FIRST), 1), WIDE * grid.padded, LANES), f32),
+            pltpu.VMEM((LANES, LANES), jnp.bfloat16),
             pltpu.SemaphoreType.DMA((4,)),
         ],
         compiler_params=pltpu.CompilerParams(vmem_limit_bytes=20 * MIB),
@@ -468,7 +494,7 @@
 def evolve_kernel(
     probes, inner, coef_in, strip_coef_in, start_in, after_one_in, x_a, x_b, c_a, c_b,
     halves, gram, coef, strip_coef, start, after_one, edges, weights,
-    wraps_of, state, later, flux, slope, grid_state, total,
+    wraps_of, state, later, flux, slope, field_slope, grid_state, total,
 ):
     fields, count, rows, _ = probes.shape
     grid = Grid(rows)
@@ -503,13 +529,16 @@
 
     def strip_body(g, carry):
         mine = flux.at[0]
-        strip_velocities(grid.around, grid.outer, g, start, after_one, strip_coef, mine, edges, 0)
+        strip_velocities(grid.outer, grid.outer, g, start, after_one, strip_coef, mine, edges, 0)
+        for at in grid.beside_outer:
+            here = pl.ds(at, 8)
+            mine[0, here] = strip_coef[0, here] * after_one[1, g, here]
         strip_heights(grid.outer, g, after_one, strip_coef, mine)
-        strip_velocities(grid.tiles, [], g, after_one, None, strip_coef, mine, edges, 4)
+        strip_velocities(grid.tiles, [], g, after_one, None, strip_coef, mine, edges, 4, lack=SECOND)
         return carry
 
     lax.fori_loop(0, groups, strip_body, 0)
-    near = 24
+    near = 16
 
     def body(i, carry):
         for k in range(WIDE):
@@ -523,7 +552,7 @@
                 state[k, c, pl.ds(bottom, HALO)] = x_after(c * count + p)
                 later[k, c, pl.ds(grid.middle[0], 8 * len(grid.middle))] = inner[p, c]
             for slot in range(4 * STEPS):
-                for at in grid.around if slot < 4 else grid.tiles:
+                for at in grid.outer if slot < 4 else grid.tiles:
                     here = pl.ds(at, 8)
                     wraps_of[k, slot, here] = pltpu.roll(edges[slot, p // 8, here], turn_of(p), 1)
 
@@ -543,14 +572,25 @@
                 down = jnp.where(lane == 0, 0.0, pltpu.roll(value, 1, 1))
                 return up - down + jnp.where(ends(), wraps_of[k, 3, pl.ds(at, 8)], 0.0)
 
+            for at in grid.beside_outer:
+                here = pl.ds(at, 8)
+                flux[k, 0, here] = coef[0, here] * later[k, 1, here]
             velocities(
-                grid.around, lambda c: state.at[k, c], coef,
+                grid.outer, lambda c: state.at[k, c], coef,
                 lambda c, at, value: shifted(value, wraps_of[k, c, pl.ds(at, 8)]),
                 flux.at[k], write_velocity,
             )
             heights(grid.outer, coef, across, flux.at[k], write_height)
 
-        for k in range(WIDE):
+        field_products(grid, later, field_slope, weights, SECOND)
+        for k in range(WIDE):
+
+            def differences(c, at, value):
+                wrap = wraps_of[k, 4 + c, pl.ds(at, 8)]
+                if c not in SECOND:
+                    return shifted(value, wrap)
+                known = field_slope[SECOND.index(c), pl.ds(k * grid.padded + at - first, 8)]
+                return known + jnp.where(ends(), wrap, 0.0)
 
             def row(c):
                 return pl.multiple_of((c * count + WIDE * i + k) * tall, 8)
@@ -561,8 +601,7 @@
 
             velocities(
                 grid.tiles, lambda c: later.at[k, c], coef,
-                lambda c, at, value: shifted(value, wraps_of[k, 4 + c, pl.ds(at, 8)]),
-                flux.at[k], write_velocity,
+                differences, flux.at[k], write_velocity,
             )
         flux_products(grid, flux, slope, weights)
         for k in range(WIDE):
@@ -634,6 +673,7 @@
             pltpu.VMEM((WIDE, fields, height, LANES), f32),
             pltpu.VMEM((WIDE, 3, height, LANES), f32),
             pltpu.VMEM((WIDE * grid.padded, LANES), f32),
+            pltpu.VMEM((max(len(SECOND), 1), WIDE * grid.padded, LANES), f32),
             pltpu.VMEM((fields * count * grid.tall, LANES), f32),
             pltpu.VMEM((2 * count, LANES), f32),
         ],

time: 54.5 us -> 51.5 us (0.945)
  Pallas kernels: 29 us -> 26 us
    pallas_call x1, Pallas kernels: 12.3 us -> 9.73 us  [evolve(): pl.pallas_call(evolve_kernel, out_shape=(jax.ShapeDtypeStruct((fields * r...]
where the time goes in v5:
time: 51.5 us; the launch traced here: 51.3 us
  Pallas kernels  26 us (50%)
  blocking collectives  14.9 us (29%)
  starting transfers between devices  9.61 us (19%)
  between operations  0.74 us (1%)
    all_to_all x1, blocking collectives, per_device(): lax.all_to_all(jnp.broadcast_to(gram[None], (devices,) + gram.shape), ('g...  14.9 us
    pallas_call x1, Pallas kernels, evolve(): pl.pallas_call(evolve_kernel, out_shape=(jax.ShapeDtypeStruct((fields * r...  9.73 us
    pallas_call x1, Pallas kernels, middle(): pl.pallas_call(middle_kernel, out_shape=(jax.ShapeDtypeStruct((count, fie...  5.62 us
    ppermute x1, starting transfers between devices, per_device(): c_a = lax.ppermute(low_high[0], 'gx', first_pairs(nx))  4.45 us
    pallas_call x1, Pallas kernels, finish(): pl.pallas_call(functools.partial(finish_kernel, scale), out_shape=(jax.Sh...  4.23 us
    pallas_call x1, Pallas kernels, alone(): pl.pallas_call(alone_kernel, in_specs=[vmem] + [hbm] * 4, out_shape=(one,...  3.61 us
    pallas_call x1, Pallas kernels, pack(): pl.pallas_call(pack_kernel, in_specs=[pl.BlockSpec(memory_space=pltpu.HBM...  2.78 us
    ppermute x1, starting transfers between devices, per_device(): got_xa = lax.ppermute(x_a, 'gx', first_pairs(nx))  2.66 us
  transfers between devices with their start and end apart: 6, of which 0 were waited for; matrix products, arithmetic and copies ran while one was open for 0% of the time, Pallas kernels for 18%

profile of v5, /device:TPU:0, one launch (start us, length us, event | category | flops | bytes accessed | tf_op | source)
XLA Modules:
  0.0 51.3 jit_solution(14878215665699090451)
XLA Ops:
  0.6 2.8 %pack_edges.1 = (f32[100,4,128]{2,1,0:T(4,128)S(1)}, f32[100,4,128]{2,1,0:T(4,128)S(1)}, f32[4,96,128]{2,1,0:T(8,128)S(1)}, f32[4,96,128]{2,1,0:T(8,128)S(1)}, bf16[3,32,96,128]{3,2,1,0:T(8,128)(2,1)S(1)}) custom-call(bf16[3,32,96,128]{3,2,1,0:T(8,128)(2,1)} %probes.1, f32[96,128]{1,0:T(8,128)} %depth.3, f32[96,128]{1,0:T(8,128)} %east_flow.3, ...), custom_call_target="tpu_custom_call" | custom-call | tf_op jit(solution)/shard_map/pack_edges/pallas_call | solution.py:100
  3.4 0.5 %collective-permute-start = (f32[4,96,128]{2,1,0:T(8,128)S(1)}, f32[4,96,128]{2,1,0:T(8,128)S(1)}, u32[]{:S(2)}, u32[]{:S(2)}) collective-permute-start(f32[4,96,128]{2,1,0:T(8,128)S(1)} %get-tuple-element.24.to_a), channel_id=1, source_target_pairs={{0,1},{1,0},{2,3},{3,2},{4,5},{5,4},{6,7},{7,6},{8,9},{9,8},{10,11... | collective-permute-start | bytes 589832 | tf_op jit(solution)/shard_map/ppermute | solution.py:808
  3.9 0.7 %collective-permute-start.1 = (f32[4,96,128]{2,1,0:T(8,128)S(1)}, f32[4,96,128]{2,1,0:T(8,128)S(1)}, u32[]{:S(2)}, u32[]{:S(2)}) collective-permute-start(f32[4,96,128]{2,1,0:T(8,128)S(1)} %get-tuple-element.25.to_b), channel_id=1, source_target_pairs={{1,2},{2,1},{3,4},{4,3},{5,6},{6,5},{9,10},{10,9},{11,12},{12,11},... | collective-permute-start | bytes 589832 | tf_op jit(solution)/shard_map/ppermute | solution.py:807
  4.6 2.7 %collective-permute-start.2 = (f32[100,4,128]{2,1,0:T(4,128)S(1)}, f32[100,4,128]{2,1,0:T(4,128)S(1)}, u32[]{:S(2)}, u32[]{:S(2)}) collective-permute-start(f32[100,4,128]{2,1,0:T(4,128)S(1)} %get-tuple-element.30), channel_id=1, source_target_pairs={{0,8},{8,0},{16,24},{24,16},{1,9},{9,1},{17,25},{25,17},{2,10},{10... | collective-permute-start | bytes 614408 | tf_op jit(solution)/shard_map/ppermute | solution.py:810
  7.3 0.7 %collective-permute-start.3 = (f32[100,4,128]{2,1,0:T(4,128)S(1)}, f32[100,4,128]{2,1,0:T(4,128)S(1)}, u32[]{:S(2)}, u32[]{:S(2)}) collective-permute-start(f32[100,4,128]{2,1,0:T(4,128)S(1)} %get-tuple-element.31), channel_id=1, source_target_pairs={{8,16},{16,8},{9,17},{17,9},{10,18},{18,10},{11,19},{19,11},{12,20... | collective-permute-start | bytes 614408 | tf_op jit(solution)/shard_map/ppermute | solution.py:809
  7.9 3.6 %first_velocities.1 = (f32[32,104,128]{2,1,0:T(8,128)S(1)}, f32[32,104,128]{2,1,0:T(8,128)S(1)}, f32[32,104,128]{2,1,0:T(8,128)S(1)}, f32[4,120,128]{2,1,0:T(8,128)S(1)}) custom-call(bf16[3,32,96,128]{3,2,1,0:T(8,128)(2,1)S(1)} %get-tuple-element.19.probes, f32[96,128]{1,0:T(8,128)} %depth.3, f32[96,128]{1,0:T(8,128)} %east_flow.3, f32[96,128]{1,0:T(8,128)} %north_flow.3, ...), custom_call_target="tpu_custom_call" | custom-call | flops 100000000 | bytes 10000000 | tf_op jit(solution)/shard_map/first_velocities/pallas_call | solution.py:351
  11.5 0.0 collective-permute-done.from_a
  11.6 0.0 collective-permute-done.1.from_b
  11.6 4.5 %collective-permute-start.4 = (f32[4,4,4,128]{3,2,1,0:T(4,128)S(1)}, f32[4,4,4,128]{3,2,1,0:T(4,128)S(1)}, u32[]{:S(2)}, u32[]{:S(2)}) collective-permute-start(f32[4,4,4,128]{3,2,1,0:T(4,128)S(1)} %get-tuple-element.32), channel_id=1, source_target_pairs={{0,8},{8,0},{16,24},{24,16},{1,9},{9,1},{17,25},{25,17},{2,10},{10... | collective-permute-start | bytes 98312 | tf_op jit(solution)/shard_map/ppermute | solution.py:814
  16.1 0.7 %collective-permute-start.5 = (f32[4,4,4,128]{3,2,1,0:T(4,128)S(1)}, f32[4,4,4,128]{3,2,1,0:T(4,128)S(1)}, u32[]{:S(2)}, u32[]{:S(2)}) collective-permute-start(f32[4,4,4,128]{3,2,1,0:T(4,128)S(1)} %get-tuple-element.33), channel_id=1, source_target_pairs={{8,16},{16,8},{9,17},{17,9},{10,18},{18,10},{11,19},{19,11},{12,20... | collective-permute-start | bytes 98312 | tf_op jit(solution)/shard_map/ppermute | solution.py:813
  16.7 5.6 %first_step.1 = (f32[32,3,88,128]{3,2,1,0:T(8,128)S(1)}, f32[4,120,128]{2,1,0:T(8,128)S(1)}, f32[3,4,120,128]{3,2,1,0:T(8,128)S(1)}, f32[3,4,120,128]{3,2,1,0:T(8,128)S(1)}) custom-call(f32[32,104,128]{2,1,0:T(8,128)S(1)} %get-tuple-element.20.first_e.unused, f32[32,104,128]{2,1,0:T(8,128)S(1)} %get-tuple-element.21.first_n, ...), custom_call_target="tpu_custom_call" | custom-call | flops 100000000 | bytes 10000000 | tf_op jit(solution)/shard_map/first_step/pallas_call | solution.py:473
  22.3 0.0 collective-permute-done.2.x_a
  22.4 0.0 collective-permute-done.3.x_b
  22.4 0.0 collective-permute-done.4.c_a
  22.4 0.0 collective-permute-done.5.c_b
  22.4 9.7 %evolve_and_gram.1 = (bf16[36,64,1024]{2,1,0:T(8,128)(2,1)S(1)}, f32[8,128]{1,0:T(8,128)S(1)}) custom-call(bf16[3,32,96,128]{3,2,1,0:T(8,128)(2,1)S(1)} %get-tuple-element.19.probes, f32[32,3,88,128]{3,2,1,0:T(8,128)S(1)} %get-tuple-element.26.inner, f32[4,120,128]{2,1,0:T(8,128)S(1)} %get-tuple-element.23.coef.coef_in, ...), custom_call_target="tpu_custom_call" | custom-call | flops 100000000 | bytes 10000000 | tf_op jit(solution)/shard_map/evolve_and_gram/pallas_call | solution.py:658
  32.1 14.9 %all_to_all.5.grams = f32[32,8,128]{2,1,0:T(8,128)S(1)} all-to-all(f32[32,8,128]{2,1,0:T(8,128)S(1)} %broadcast_in_dim.2), channel_id=1, replica_groups=mesh['gx'=4,'gy'=8] {'gx','gy'}, dimensions={0} | all-to-all | bytes 262144 | tf_op jit(solution)/shard_map/all_to_all | solution.py:818
  47.0 4.2 %factor_and_apply.1 = (bf16[3,32,96,128]{3,2,1,0:T(8,128)(2,1)}, f32[32,32]{1,0:T(8,128)}) custom-call(f32[32,8,128]{2,1,0:T(8,128)S(1)} %all_to_all.5.grams, bf16[36,64,1024]{2,1,0:T(8,128)(2,1)S(1)} %get-tuple-element.35.halves), custom_call_target="tpu_custom_call" | custom-call | tf_op jit(solution)/shard_map/factor_and_apply/pallas_call | solution.py:774
  (2 shorter events, 0.0 us)
Async XLA Ops:
  3.4 8.1 %collective-permute-start = (f32[4,96,128]{2,1,0:T(8,128)S(1)}, f32[4,96,128]{2,1,0:T(8,128)S(1)}, u32[]{:S(2)}, u32[]{:S(2)}) collective-permute-start(f32[4,96,128]{2,1,0:T(8,128)S(1)} %get-tuple-element.24.to_a), channel_id=1, source_target_pairs={{0,1},{1,0},{2,3},{3,2},{4,5},{5,4},{6,7},{7,6},{8,9},{9,8},{10,11... | collective-permute-start | bytes 589832 | tf_op jit(solution)/shard_map/ppermute | solution.py:808
  3.9 7.6 %collective-permute-start.1 = (f32[4,96,128]{2,1,0:T(8,128)S(1)}, f32[4,96,128]{2,1,0:T(8,128)S(1)}, u32[]{:S(2)}, u32[]{:S(2)}) collective-permute-start(f32[4,96,128]{2,1,0:T(8,128)S(1)} %get-tuple-element.25.to_b), channel_id=1, source_target_pairs={{1,2},{2,1},{3,4},{4,3},{5,6},{6,5},{9,10},{10,9},{11,12},{12,11},... | collective-permute-start | bytes 589832 | tf_op jit(solution)/shard_map/ppermute | solution.py:807
  4.6 17.7 %collective-permute-start.2 = (f32[100,4,128]{2,1,0:T(4,128)S(1)}, f32[100,4,128]{2,1,0:T(4,128)S(1)}, u32[]{:S(2)}, u32[]{:S(2)}) collective-permute-start(f32[100,4,128]{2,1,0:T(4,128)S(1)} %get-tuple-element.30), channel_id=1, source_target_pairs={{0,8},{8,0},{16,24},{24,16},{1,9},{9,1},{17,25},{25,17},{2,10},{10... | collective-permute-start | bytes 614408 | tf_op jit(solution)/shard_map/ppermute | solution.py:810
  7.3 15.1 %collective-permute-start.3 = (f32[100,4,128]{2,1,0:T(4,128)S(1)}, f32[100,4,128]{2,1,0:T(4,128)S(1)}, u32[]{:S(2)}, u32[]{:S(2)}) collective-permute-start(f32[100,4,128]{2,1,0:T(4,128)S(1)} %get-tuple-element.31), channel_id=1, source_target_pairs={{8,16},{16,8},{9,17},{17,9},{10,18},{18,10},{11,19},{19,11},{12,20... | collective-permute-start | bytes 614408 | tf_op jit(solution)/shard_map/ppermute | solution.py:809
  11.6 10.8 %collective-permute-start.4 = (f32[4,4,4,128]{3,2,1,0:T(4,128)S(1)}, f32[4,4,4,128]{3,2,1,0:T(4,128)S(1)}, u32[]{:S(2)}, u32[]{:S(2)}) collective-permute-start(f32[4,4,4,128]{3,2,1,0:T(4,128)S(1)} %get-tuple-element.32), channel_id=1, source_target_pairs={{0,8},{8,0},{16,24},{24,16},{1,9},{9,1},{17,25},{25,17},{2,10},{10... | collective-permute-start | bytes 98312 | tf_op jit(solution)/shard_map/ppermute | solution.py:814
  16.1 6.3 %collective-permute-start.5 = (f32[4,4,4,128]{3,2,1,0:T(4,128)S(1)}, f32[4,4,4,128]{3,2,1,0:T(4,128)S(1)}, u32[]{:S(2)}, u32[]{:S(2)}) collective-permute-start(f32[4,4,4,128]{3,2,1,0:T(4,128)S(1)} %get-tuple-element.33), channel_id=1, source_target_pairs={{8,16},{16,8},{9,17},{17,9},{10,18},{18,10},{11,19},{19,11},{12,20... | collective-permute-start | bytes 98312 | tf_op jit(solution)/shard_map/ppermute | solution.py:813

commit v6 on v5

--- a/solution.py
+++ b/solution.py
@@ -19,7 +19,7 @@
 
 MIB = 1024 * 1024
 BLOCK = 8
-PARTS = 2
+PARTS = 1
 FIRST = (0, 1)
 SECOND = (0, 1, 2)
 PIVOTS = 8
@@ -758,7 +758,7 @@
                 staged[c, q] = grid_out[pl.ds(at, rows)].astype(jnp.bfloat16)
                 return carry
 
-            lax.fori_loop(0, count // PARTS, store, 0, unroll=4)
+            lax.fori_loop(0, count // PARTS, store, 0, unroll=True)
             copies.append(
                 pltpu.make_async_copy(
                     staged.at[c, these], basis.at[c, these], sems.at[c * PARTS + part_of]

time: 51.5 us -> 51 us (level)
  no operation moved by 1% of the time
where the time goes in v6:
time: 51 us; the launch traced here: 50.8 us
  Pallas kernels  25.5 us (50%)
  blocking collectives  14.9 us (29%)
  starting transfers between devices  9.61 us (19%)
  between operations  0.74 us (1%)
    all_to_all x1, blocking collectives, per_device(): lax.all_to_all(jnp.broadcast_to(gram[None], (devices,) + gram.shape), ('g...  14.9 us
    pallas_call x1, Pallas kernels, evolve(): pl.pallas_call(evolve_kernel, out_shape=(jax.ShapeDtypeStruct((fields * r...  9.73 us
    pallas_call x1, Pallas kernels, middle(): pl.pallas_call(middle_kernel, out_shape=(jax.ShapeDtypeStruct((count, fie...  5.62 us
    ppermute x1, starting transfers between devices, per_device(): c_a = lax.ppermute(low_high[0], 'gx', first_pairs(nx))  4.45 us
    pallas_call x1, Pallas kernels, finish(): pl.pallas_call(functools.partial(finish_kernel, scale), out_shape=(jax.Sh...  3.76 us
    pallas_call x1, Pallas kernels, alone(): pl.pallas_call(alone_kernel, in_specs=[vmem] + [hbm] * 4, out_shape=(one,...  3.61 us
    pallas_call x1, Pallas kernels, pack(): pl.pallas_call(pack_kernel, in_specs=[pl.BlockSpec(memory_space=pltpu.HBM...  2.78 us
    ppermute x1, starting transfers between devices, per_device(): got_xa = lax.ppermute(x_a, 'gx', first_pairs(nx))  2.66 us
  transfers between devices with their start and end apart: 6, of which 0 were waited for; matrix products, arithmetic and copies ran while one was open for 0% of the time, Pallas kernels for 18%

profile of v6, /device:TPU:0, one launch (start us, length us, event | category | flops | bytes accessed | tf_op | source)
XLA Modules:
  0.0 50.8 jit_solution(12284893875583975256)
XLA Ops:
  0.6 2.8 %pack_edges.1 = (f32[100,4,128]{2,1,0:T(4,128)S(1)}, f32[100,4,128]{2,1,0:T(4,128)S(1)}, f32[4,96,128]{2,1,0:T(8,128)S(1)}, f32[4,96,128]{2,1,0:T(8,128)S(1)}, bf16[3,32,96,128]{3,2,1,0:T(8,128)(2,1)S(1)}) custom-call(bf16[3,32,96,128]{3,2,1,0:T(8,128)(2,1)} %probes.1, f32[96,128]{1,0:T(8,128)} %depth.3, f32[96,128]{1,0:T(8,128)} %east_flow.3, ...), custom_call_target="tpu_custom_call" | custom-call | tf_op jit(solution)/shard_map/pack_edges/pallas_call | solution.py:100
  3.4 0.5 %collective-permute-start = (f32[4,96,128]{2,1,0:T(8,128)S(1)}, f32[4,96,128]{2,1,0:T(8,128)S(1)}, u32[]{:S(2)}, u32[]{:S(2)}) collective-permute-start(f32[4,96,128]{2,1,0:T(8,128)S(1)} %get-tuple-element.24.to_a), channel_id=1, source_target_pairs={{0,1},{1,0},{2,3},{3,2},{4,5},{5,4},{6,7},{7,6},{8,9},{9,8},{10,11... | collective-permute-start | bytes 589832 | tf_op jit(solution)/shard_map/ppermute | solution.py:808
  3.9 0.7 %collective-permute-start.1 = (f32[4,96,128]{2,1,0:T(8,128)S(1)}, f32[4,96,128]{2,1,0:T(8,128)S(1)}, u32[]{:S(2)}, u32[]{:S(2)}) collective-permute-start(f32[4,96,128]{2,1,0:T(8,128)S(1)} %get-tuple-element.25.to_b), channel_id=1, source_target_pairs={{1,2},{2,1},{3,4},{4,3},{5,6},{6,5},{9,10},{10,9},{11,12},{12,11},... | collective-permute-start | bytes 589832 | tf_op jit(solution)/shard_map/ppermute | solution.py:807
  4.6 2.7 %collective-permute-start.2 = (f32[100,4,128]{2,1,0:T(4,128)S(1)}, f32[100,4,128]{2,1,0:T(4,128)S(1)}, u32[]{:S(2)}, u32[]{:S(2)}) collective-permute-start(f32[100,4,128]{2,1,0:T(4,128)S(1)} %get-tuple-element.30), channel_id=1, source_target_pairs={{0,8},{8,0},{16,24},{24,16},{1,9},{9,1},{17,25},{25,17},{2,10},{10... | collective-permute-start | bytes 614408 | tf_op jit(solution)/shard_map/ppermute | solution.py:810
  7.3 0.7 %collective-permute-start.3 = (f32[100,4,128]{2,1,0:T(4,128)S(1)}, f32[100,4,128]{2,1,0:T(4,128)S(1)}, u32[]{:S(2)}, u32[]{:S(2)}) collective-permute-start(f32[100,4,128]{2,1,0:T(4,128)S(1)} %get-tuple-element.31), channel_id=1, source_target_pairs={{8,16},{16,8},{9,17},{17,9},{10,18},{18,10},{11,19},{19,11},{12,20... | collective-permute-start | bytes 614408 | tf_op jit(solution)/shard_map/ppermute | solution.py:809
  7.9 3.6 %first_velocities.1 = (f32[32,104,128]{2,1,0:T(8,128)S(1)}, f32[32,104,128]{2,1,0:T(8,128)S(1)}, f32[32,104,128]{2,1,0:T(8,128)S(1)}, f32[4,120,128]{2,1,0:T(8,128)S(1)}) custom-call(bf16[3,32,96,128]{3,2,1,0:T(8,128)(2,1)S(1)} %get-tuple-element.19.probes, f32[96,128]{1,0:T(8,128)} %depth.3, f32[96,128]{1,0:T(8,128)} %east_flow.3, f32[96,128]{1,0:T(8,128)} %north_flow.3, ...), custom_call_target="tpu_custom_call" | custom-call | flops 100000000 | bytes 10000000 | tf_op jit(solution)/shard_map/first_velocities/pallas_call | solution.py:351
  11.5 0.0 collective-permute-done.from_a
  11.6 0.0 collective-permute-done.1.from_b
  11.6 4.5 %collective-permute-start.4 = (f32[4,4,4,128]{3,2,1,0:T(4,128)S(1)}, f32[4,4,4,128]{3,2,1,0:T(4,128)S(1)}, u32[]{:S(2)}, u32[]{:S(2)}) collective-permute-start(f32[4,4,4,128]{3,2,1,0:T(4,128)S(1)} %get-tuple-element.32), channel_id=1, source_target_pairs={{0,8},{8,0},{16,24},{24,16},{1,9},{9,1},{17,25},{25,17},{2,10},{10... | collective-permute-start | bytes 98312 | tf_op jit(solution)/shard_map/ppermute | solution.py:814
  16.1 0.7 %collective-permute-start.5 = (f32[4,4,4,128]{3,2,1,0:T(4,128)S(1)}, f32[4,4,4,128]{3,2,1,0:T(4,128)S(1)}, u32[]{:S(2)}, u32[]{:S(2)}) collective-permute-start(f32[4,4,4,128]{3,2,1,0:T(4,128)S(1)} %get-tuple-element.33), channel_id=1, source_target_pairs={{8,16},{16,8},{9,17},{17,9},{10,18},{18,10},{11,19},{19,11},{12,20... | collective-permute-start | bytes 98312 | tf_op jit(solution)/shard_map/ppermute | solution.py:813
  16.7 5.6 %first_step.1 = (f32[32,3,88,128]{3,2,1,0:T(8,128)S(1)}, f32[4,120,128]{2,1,0:T(8,128)S(1)}, f32[3,4,120,128]{3,2,1,0:T(8,128)S(1)}, f32[3,4,120,128]{3,2,1,0:T(8,128)S(1)}) custom-call(f32[32,104,128]{2,1,0:T(8,128)S(1)} %get-tuple-element.20.first_e.unused, f32[32,104,128]{2,1,0:T(8,128)S(1)} %get-tuple-element.21.first_n, ...), custom_call_target="tpu_custom_call" | custom-call | flops 100000000 | bytes 10000000 | tf_op jit(solution)/shard_map/first_step/pallas_call | solution.py:473
  22.3 0.0 collective-permute-done.2.x_a
  22.4 0.0 collective-permute-done.3.x_b
  22.4 0.0 collective-permute-done.4.c_a
  22.4 0.0 collective-permute-done.5.c_b
  22.4 9.7 %evolve_and_gram.1 = (bf16[36,64,1024]{2,1,0:T(8,128)(2,1)S(1)}, f32[8,128]{1,0:T(8,128)S(1)}) custom-call(bf16[3,32,96,128]{3,2,1,0:T(8,128)(2,1)S(1)} %get-tuple-element.19.probes, f32[32,3,88,128]{3,2,1,0:T(8,128)S(1)} %get-tuple-element.26.inner, f32[4,120,128]{2,1,0:T(8,128)S(1)} %get-tuple-element.23.coef.coef_in, ...), custom_call_target="tpu_custom_call" | custom-call | flops 100000000 | bytes 10000000 | tf_op jit(solution)/shard_map/evolve_and_gram/pallas_call | solution.py:658
  32.1 14.9 %all_to_all.5.grams = f32[32,8,128]{2,1,0:T(8,128)S(1)} all-to-all(f32[32,8,128]{2,1,0:T(8,128)S(1)} %broadcast_in_dim.2), channel_id=1, replica_groups=mesh['gx'=4,'gy'=8] {'gx','gy'}, dimensions={0} | all-to-all | bytes 262144 | tf_op jit(solution)/shard_map/all_to_all | solution.py:818
  47.0 3.8 %factor_and_apply.1 = (bf16[3,32,96,128]{3,2,1,0:T(8,128)(2,1)}, f32[32,32]{1,0:T(8,128)}) custom-call(f32[32,8,128]{2,1,0:T(8,128)S(1)} %all_to_all.5.grams, bf16[36,64,1024]{2,1,0:T(8,128)(2,1)S(1)} %get-tuple-element.35.halves), custom_call_target="tpu_custom_call" | custom-call | tf_op jit(solution)/shard_map/factor_and_apply/pallas_call | solution.py:774
  (2 shorter events, 0.0 us)
Async XLA Ops:
  3.4 8.1 %collective-permute-start = (f32[4,96,128]{2,1,0:T(8,128)S(1)}, f32[4,96,128]{2,1,0:T(8,128)S(1)}, u32[]{:S(2)}, u32[]{:S(2)}) collective-permute-start(f32[4,96,128]{2,1,0:T(8,128)S(1)} %get-tuple-element.24.to_a), channel_id=1, source_target_pairs={{0,1},{1,0},{2,3},{3,2},{4,5},{5,4},{6,7},{7,6},{8,9},{9,8},{10,11... | collective-permute-start | bytes 589832 | tf_op jit(solution)/shard_map/ppermute | solution.py:808
  3.9 7.6 %collective-permute-start.1 = (f32[4,96,128]{2,1,0:T(8,128)S(1)}, f32[4,96,128]{2,1,0:T(8,128)S(1)}, u32[]{:S(2)}, u32[]{:S(2)}) collective-permute-start(f32[4,96,128]{2,1,0:T(8,128)S(1)} %get-tuple-element.25.to_b), channel_id=1, source_target_pairs={{1,2},{2,1},{3,4},{4,3},{5,6},{6,5},{9,10},{10,9},{11,12},{12,11},... | collective-permute-start | bytes 589832 | tf_op jit(solution)/shard_map/ppermute | solution.py:807
  4.6 17.7 %collective-permute-start.2 = (f32[100,4,128]{2,1,0:T(4,128)S(1)}, f32[100,4,128]{2,1,0:T(4,128)S(1)}, u32[]{:S(2)}, u32[]{:S(2)}) collective-permute-start(f32[100,4,128]{2,1,0:T(4,128)S(1)} %get-tuple-element.30), channel_id=1, source_target_pairs={{0,8},{8,0},{16,24},{24,16},{1,9},{9,1},{17,25},{25,17},{2,10},{10... | collective-permute-start | bytes 614408 | tf_op jit(solution)/shard_map/ppermute | solution.py:810
  7.3 15.1 %collective-permute-start.3 = (f32[100,4,128]{2,1,0:T(4,128)S(1)}, f32[100,4,128]{2,1,0:T(4,128)S(1)}, u32[]{:S(2)}, u32[]{:S(2)}) collective-permute-start(f32[100,4,128]{2,1,0:T(4,128)S(1)} %get-tuple-element.31), channel_id=1, source_target_pairs={{8,16},{16,8},{9,17},{17,9},{10,18},{18,10},{11,19},{19,11},{12,20... | collective-permute-start | bytes 614408 | tf_op jit(solution)/shard_map/ppermute | solution.py:809
  11.6 10.8 %collective-permute-start.4 = (f32[4,4,4,128]{3,2,1,0:T(4,128)S(1)}, f32[4,4,4,128]{3,2,1,0:T(4,128)S(1)}, u32[]{:S(2)}, u32[]{:S(2)}) collective-permute-start(f32[4,4,4,128]{3,2,1,0:T(4,128)S(1)} %get-tuple-element.32), channel_id=1, source_target_pairs={{0,8},{8,0},{16,24},{24,16},{1,9},{9,1},{17,25},{25,17},{2,10},{10... | collective-permute-start | bytes 98312 | tf_op jit(solution)/shard_map/ppermute | solution.py:814
  16.1 6.3 %collective-permute-start.5 = (f32[4,4,4,128]{3,2,1,0:T(4,128)S(1)}, f32[4,4,4,128]{3,2,1,0:T(4,128)S(1)}, u32[]{:S(2)}, u32[]{:S(2)}) collective-permute-start(f32[4,4,4,128]{3,2,1,0:T(4,128)S(1)} %get-tuple-element.33), channel_id=1, source_target_pairs={{8,16},{16,8},{9,17},{17,9},{10,18},{18,10},{11,19},{19,11},{12,20... | collective-permute-start | bytes 98312 | tf_op jit(solution)/shard_map/ppermute | solution.py:813
